TPU v7x, 256 devices: a whole 4x4x8 slice. The times are simulated.
256 devices in a mesh: dp: 32 (over z_lo, x, core), vocab: 8 (over y, z_hi).
Axes of the slice: x: 4, y: 4, z: 8 (z_hi: 2, z_lo: 4; z = z_hi * 4 + z_lo), core: 2. Of those that a mesh axis runs over, the one named last changes fastest.
Arguments:
- teacher_rows: bfloat16 [256, 16384], P('vocab', 'dp')
- teacher_gain: bfloat16 [16384], replicated, may hold values from 0.5 to 1.5
- teacher_head: bfloat16 [16384, 65536], P(None, ('dp', 'vocab'))
- student_rows: bfloat16 [256, 8192], P('dp', 'vocab')
- student_gain: bfloat16 [8192], replicated, may hold values from 0.5 to 1.5
- student_head: bfloat16 [8192, 65536], P(None, ('dp', 'vocab'))
- sampled_ids: int32 [256], replicated, may hold values from 0 to 65535
- response_mask: int32 [256], replicated, may hold values from 0 to 1, as said below
Outputs:
- distill_loss: float32 [], replicated
- student_rows_grad: bfloat16 [256, 8192], P('dp', 'vocab')
- student_gain_grad: float32 [8192], P('vocab')
Inputs may be any that keep to these rules, and one draw needn't show every extreme that they name: response_mask[255] is 1.
All inputs are finite; a program needn't handle non-finite values.
Results may differ from a plain program's by a relative error of at most 0.0067.
Values may be sent and summed in bfloat16 or wider, within the bound.
A program may use at most 128 MiB of HBM per device.

v0:
```python
import math

import jax
import jax.numpy as jnp
from jax import lax
from jax.sharding import PartitionSpec as P

EPSILON = 1e-05
MIX_WEIGHT = 0.3
NLL_WEIGHT = 0.03
LOSS_SCALE = 8192.0


def rms_inverse(hidden_rows):
    widened = hidden_rows.astype(jnp.float32)
    return lax.rsqrt(jnp.mean(widened * widened, axis=1, keepdims=True) + EPSILON)


def shards(
    teacher_rows,
    teacher_gain,
    teacher_head,
    student_rows,
    student_gain,
    student_head,
    sampled_ids,
    response_mask,
):
    teacher_wide = lax.all_gather(teacher_rows, "dp", axis=1, tiled=True)
    teacher_full = lax.all_gather(teacher_wide, "vocab", axis=0, tiled=True)
    student_wide = lax.all_gather(student_rows, "vocab", axis=1, tiled=True)
    student_full = lax.all_gather(student_wide, "dp", axis=0, tiled=True)
    teacher_inv = rms_inverse(teacher_full)
    teacher_normed = (
        teacher_full.astype(jnp.float32) * teacher_inv * teacher_gain.astype(jnp.float32)
    ).astype(jnp.bfloat16)
    teacher_logits = jnp.dot(teacher_normed, teacher_head, preferred_element_type=jnp.float32)
    student_inv = rms_inverse(student_full)
    student_normed = (
        student_full.astype(jnp.float32) * student_inv * student_gain.astype(jnp.float32)
    ).astype(jnp.bfloat16)
    student_logits = jnp.dot(student_normed, student_head, preferred_element_type=jnp.float32)
    shard_width = student_head.shape[1]
    column_start = (
        lax.axis_index("dp") * lax.axis_size("vocab") + lax.axis_index("vocab")
    ) * shard_width
    columns = column_start + lax.broadcasted_iota(jnp.int32, student_logits.shape, 1)
    onehot = (columns == sampled_ids[:, None]).astype(jnp.float32)
    picked_part = jnp.sum(onehot * student_logits, axis=1)
    teacher_local_top = jnp.max(teacher_logits, axis=1)
    student_local_top = jnp.max(student_logits, axis=1)
    teacher_top, student_top = lax.pmax((teacher_local_top, student_local_top), ("dp", "vocab"))
    teacher_total, student_total, picked = lax.psum(
        (
            jnp.sum(jnp.exp(teacher_logits - teacher_top[:, None]), axis=1),
            jnp.sum(jnp.exp(student_logits - student_top[:, None]), axis=1),
            picked_part,
        ),
        ("dp", "vocab"),
    )
    teacher_lse = teacher_top + jnp.log(teacher_total)
    student_lse = student_top + jnp.log(student_total)
    teacher_logp = teacher_logits - teacher_lse[:, None]
    student_logp = student_logits - student_lse[:, None]
    mix_logp = jnp.logaddexp(
        math.log(MIX_WEIGHT) + teacher_logp, math.log(1.0 - MIX_WEIGHT) + student_logp
    )
    teacher_prob = jnp.exp(teacher_logp)
    student_prob = jnp.exp(student_logp)
    student_gap = student_logp - mix_logp
    jsd_part = jnp.sum(
        MIX_WEIGHT * teacher_prob * (teacher_logp - mix_logp)
        + (1.0 - MIX_WEIGHT) * student_prob * student_gap,
        axis=1,
    )
    kl_part = jnp.sum(student_prob * student_gap, axis=1)
    jsd, kl_student = lax.psum((jsd_part, kl_part), ("dp", "vocab"))
    weights = response_mask.astype(jnp.float32)
    token_count = jnp.sum(weights)
    distill_loss = jnp.sum(weights * (jsd + NLL_WEIGHT * (student_lse - picked))) / token_count
    row_scale = (LOSS_SCALE * weights / token_count)[:, None]
    logit_grad = (
        row_scale
        * (
            student_prob
            * ((1.0 - MIX_WEIGHT) * student_gap - (1.0 - MIX_WEIGHT) * kl_student[:, None])
            + NLL_WEIGHT * (student_prob - onehot)
        )
    ).astype(jnp.bfloat16)
    own_rows = student_rows.shape[0]
    row_offset = lax.axis_index("dp") * own_rows
    inv_own = lax.dynamic_slice_in_dim(student_inv, row_offset, own_rows, 0)
    feature_count = student_rows.shape[1]
    feature_start = lax.axis_index("vocab") * feature_count
    full_width = student_gain.shape[0]
    gain_own = lax.dynamic_slice_in_dim(student_gain, feature_start, feature_count, 0).astype(
        jnp.float32
    )
    scaled_own = student_rows.astype(jnp.float32) * inv_own
    normed_part = lax.psum_scatter(
        lax.dot_general(
            logit_grad, student_head, (((1,), (1,)), ((), ())), preferred_element_type=jnp.float32
        ),
        "dp",
        scatter_dimension=0,
        tiled=True,
    )
    normed_grad = lax.psum_scatter(normed_part, "vocab", scatter_dimension=1, tiled=True)
    scaled_grad = normed_grad * gain_own
    row_dot = (
        lax.psum(jnp.sum(scaled_grad * scaled_own, axis=1, keepdims=True), "vocab") / full_width
    )
    student_gain_grad = lax.psum(jnp.sum(normed_grad * scaled_own, axis=0), "dp")
    student_rows_grad = (inv_own * (scaled_grad - scaled_own * row_dot)).astype(jnp.bfloat16)
    return (distill_loss, student_rows_grad, student_gain_grad)


def solution(mesh):
    return jax.shard_map(
        shards,
        mesh=mesh,
        in_specs=(
            P("vocab", "dp"),
            P(),
            P(None, ("dp", "vocab")),
            P("dp", "vocab"),
            P(),
            P(None, ("dp", "vocab")),
            P(),
            P(),
        ),
        out_specs=(P(), P("dp", "vocab"), P("vocab")),
        check_vma=False,
    )
```

profile of v0, /device:TPU:32, one launch (start us, length us, event | category | flops | bytes accessed | tf_op | source)
XLA Modules:
  0.0 881.5 jit_solution(10581227334421390940)
XLA Ops:
  7.2 0.0 all-gather.4.cloned.1.call-start
  7.2 0.7 all-gather.4.cloned.1.call-update
  7.9 0.0 all-gather.8.cloned.1.call-start
  7.9 47.0 %all_gather.14 = bf16[8,8192]{1,0:T(8,128)(2,1)} all-gather(bf16[8,1024]{1,0:T(8,128)(2,1)} %param.11), channel_id=1, replica_groups=mesh['dp'=32,'vocab'=8] {'vocab'}, dimensions={1}, use_global_device_ids=true | all-gather | bytes 147456 | tf_op jit(solution)/shard_map/all_gather | solution.py:31
  54.9 0.0 all-gather.8.cloned.1.call-update
  54.9 0.0 all-gather.6.cloned.1.call-start
  55.0 16.0 %all-gather.4.cloned.1.call-done = bf16[32,16384]{1,0:T(8,128)(2,1)} async-done(((bf16[32,512]{1,0:T(8,128)(2,1)}), bf16[32,16384]{1,0:T(8,128)(2,1)}) %all-gather.4.cloned.1.call-update) | async-done | bytes 1048592 | tf_op jit(solution)/shard_map/all_gather | solution.py:29
  71.0 0.0 all-gather.6.cloned.1.call-update
  71.0 0.0 reduce-scatter.3.cloned.1.call-start
  71.1 0.7 convert_element_type.43
  71.8 0.8 convert_element_type.40
  72.6 62.4 %all-gather.8.cloned.1.call-done = bf16[256,8192]{1,0:T(8,128)(2,1)} async-done(((bf16[8,8192]{1,0:T(8,128)(2,1)}), bf16[256,8192]{1,0:T(8,128)(2,1)}) %all-gather.8.cloned.1.call-update) | async-done | bytes 4194320 | tf_op jit(solution)/shard_map/all_gather | solution.py:32
  134.9 3.1 fusion.3
  138.1 5.5 fusion.33
  143.6 165.0 %all-gather.6.cloned.1.call-done = bf16[256,16384]{1,0:T(8,128)(2,1)} async-done(((bf16[32,16384]{1,0:T(8,128)(2,1)}), bf16[256,16384]{1,0:T(8,128)(2,1)}) %all-gather.6.cloned.1.call-update) | async-done | bytes 8388624 | tf_op jit(solution)/shard_map/all_gather | solution.py:30
  308.6 5.1 fusion
  313.7 0.0 copy-start.1
  313.7 0.0 copy-start.2
  313.7 9.8 %fusion.34 = (f32[256]{0:T(256)S(1)}, f32[256,256]{0,1:T(8,128)S(1)}) fusion(bf16[16384,256]{1,0:T(8,128)(2,1)} %param.10, bf16[256,16384]{1,0:T(8,128)(2,1)} %all-gather.6.cloned.1.call-done, f32[16384]{0:T(1024)S(1)} %convert_element_type.40, f32[256]{0:T(256)S(1)} %add_rsqrt_fusion.1), kind=kOutput, calls=%fused_computation.58 | convolution fusion | flops 2164326144 | bytes 17106944 | tf_op jit(solution)/shard_map/dot_general | solution.py:37
  323.5 75.9 %all-reduce.2 = (f32[256]{0:T(256)S(1)}, f32[256]{0:T(256)S(1)}) all-reduce(f32[256]{0:T(256)S(1)} %get-tuple-element.17, f32[256]{0:T(256)S(1)} %get-tuple-element.19), channel_id=1, replica_groups=mesh['dp'=32,'vocab'=8] {'dp','vocab'}, use_global_device_ids=true, to_apply=%region_7.0 | all-reduce | flops 512 | bytes 4096 | tf_op jit(solution)/shard_map/pmax | solution.py:52
  399.4 0.1 exponential_reduce_fusion
  399.5 72.9 %all-reduce.1 = (f32[256]{0:T(256)S(1)}, f32[256]{0:T(256)S(1)}) all-reduce(f32[256]{0:T(256)S(1)} %get-tuple-element.21, f32[256]{0:T(256)S(1)} %get-tuple-element.22), channel_id=1, replica_groups=mesh['dp'=32,'vocab'=8] {'dp','vocab'}, use_global_device_ids=true, to_apply=%region_9.0 | all-reduce | flops 512 | bytes 4096 | tf_op jit(solution)/shard_map/psum | solution.py:53
  472.4 0.0 copy-done.1
  472.4 0.4 multiply_reduce_fusion
  472.8 74.4 %all-reduce = (f32[256]{0:T(256)S(1)}, f32[256]{0:T(256)S(1)}, f32[256]{0:T(256)S(1)}) all-reduce(f32[256]{0:T(256)S(1)} %get-tuple-element.4, f32[256]{0:T(256)S(1)} %get-tuple-element.5, f32[256]{0:T(256)S(1)} %get-tuple-element.3), channel_id=1, replica_groups=mesh['dp'=32,'vocab'=8] {'dp','vocab'}, use_global_device_ids=true, to_apply=%region_11.0 | all-reduce | flops 768 | bytes 6144 | tf_op jit(solution)/shard_map/psum | solution.py:77
  547.2 0.0 copy-done.2
  547.2 0.6 convert_reduce_fusion
  547.8 0.6 multiply_divide_fusion
  548.5 0.0 copy-start
  548.5 7.0 fusion.20
  555.5 0.0 reduce-scatter.3.cloned.1.call-update
  555.5 0.0 reduce-scatter.5.cloned.1.call-start
  555.6 131.2 %reduce-scatter.3.cloned.1.call-done = f32[8,8192]{1,0:T(8,128)} async-done(((f32[256,8192]{1,0:T(8,128)}), f32[8,8192]{1,0:T(8,128)}) %reduce-scatter.3.cloned.1.call-update) | async-done | bytes 262160 | tf_op jit(solution)/shard_map/reduce_scatter | solution.py:100
  686.8 0.0 reduce-scatter.5.cloned.1.call-update
  686.8 0.7 dynamic-slice_convert_fusion
  687.5 0.1 dynamic-slice.3
  688.9 101.3 %reduce-scatter.5.cloned.1.call-done = f32[8,1024]{1,0:T(8,128)} async-done(((f32[8,8192]{1,0:T(8,128)}), f32[8,1024]{1,0:T(8,128)}) %reduce-scatter.5.cloned.1.call-update) | async-done | bytes 32784 | tf_op jit(solution)/shard_map/reduce_scatter | solution.py:108
  790.2 0.0 copy-done
  790.2 1.0 multiply_reduce_fusion.1
  791.2 54.7 %psum.55 = f32[1024]{0:T(1024)} all-reduce(f32[1024]{0:T(1024)S(1)} %get-tuple-element.6), channel_id=1, replica_groups=mesh['dp'=32,'vocab'=8] {'dp'}, use_global_device_ids=true, to_apply=%region_23.0 | all-reduce | flops 1024 | bytes 8192 | tf_op jit(solution)/shard_map/psum | solution.py:113
  845.9 26.5 %psum.54 = f32[8,1]{0,1:T(1,128)S(1)} all-reduce(f32[8,1]{0,1:T(1,128)S(1)} %bitcast.6), channel_id=1, replica_groups=mesh['dp'=32,'vocab'=8] {'vocab'}, use_global_device_ids=true, to_apply=%region_21.0 | all-reduce | flops 8 | bytes 64 | tf_op jit(solution)/shard_map/psum | solution.py:111
  872.4 1.4 multiply_convert_fusion
  (7 shorter events, 0.0 us)
Async XLA Ops:
  7.2 63.9 %all-gather.4.cloned.1.call-start = ((), (), s32[]{:S(2)}) async-start(), calls=%async_computation.2 | async-start | bytes 1081344 | tf_op jit(solution)/shard_map/all_gather | solution.py:29
  7.9 127.0 %all-gather.8.cloned.1.call-start = ((), (), s32[]{:S(2)}) async-start(), calls=%async_computation.4 | async-start | bytes 4325376 | tf_op jit(solution)/shard_map/all_gather | solution.py:32
  54.9 253.6 %all-gather.6.cloned.1.call-start = ((), (), s32[]{:S(2)}) async-start(), calls=%async_computation.3 | async-start | bytes 9437184 | tf_op jit(solution)/shard_map/all_gather | solution.py:30
  71.0 615.8 %reduce-scatter.3.cloned.1.call-start = ((), (), s32[]{:S(2)}) async-start(), calls=%async_computation.5 | async-start | bytes 8650752 | tf_op jit(solution)/shard_map/reduce_scatter | solution.py:100
  313.7 158.7 %copy-start.1 = (s32[256]{0:T(256)S(1)}, s32[256]{0:T(256)}, u32[]{:S(2)}) copy-start(s32[256]{0:T(256)} %param.14) | copy-start | bytes 3076
  313.7 233.5 %copy-start.2 = (s32[256]{0:T(256)S(1)}, s32[256]{0:T(256)}, u32[]{:S(2)}) copy-start(s32[256]{0:T(256)} %param.15) | copy-start | bytes 3076
  548.5 241.8 %copy-start = (bf16[8,1024]{1,0:T(8,128)(2,1)S(1)}, bf16[8,1024]{1,0:T(8,128)(2,1)}, u32[]{:S(2)}) copy-start(bf16[8,1024]{1,0:T(8,128)(2,1)} %param.11) | copy-start | bytes 49156
  555.5 234.7 %reduce-scatter.5.cloned.1.call-start = ((), (), s32[]{:S(2)}) async-start(), calls=%async_computation.6 | async-start | bytes 294912 | tf_op jit(solution)/shard_map/reduce_scatter | solution.py:108
Sparse Core Ops, SparseCore 0:
  9.9 61.1 all-gather.3
  72.9 62.0 all-gather.7
  137.6 170.9 all-gather.5
  555.6 131.1 reduce-scatter.2
  690.5 99.6 reduce-scatter.4
where the time goes:
time: 897 us; the launch traced here: 881 us
  waiting for transfers between devices  477 us (53%)
  blocking collectives  351 us (39%)
  matrix products  22.3 us (2%)
  between operations  16.3 us (2%)
  other arithmetic  14.6 us (2%)
    all_gather x1, waiting for transfers between devices, shards(): teacher_full = lax.all_gather(teacher_wide, 'vocab', axis=0, tiled=True)  165 us
    reduce_scatter x1, waiting for transfers between devices, shards(): lax.psum_scatter(lax.dot_general(logit_grad, student_head, (((1,), (1,)),...  131 us
    reduce_scatter x1, waiting for transfers between devices, shards(): lax.psum_scatter(normed_part, 'vocab', scatter_dimension=1, tiled=True)  101 us
    pmax x1, blocking collectives, shards(): lax.pmax((teacher_local_top, student_local_top), ('dp', 'vocab'))  75.9 us
    psum x1, blocking collectives, shards(): jsd, kl_student = lax.psum((jsd_part, kl_part), ('dp', 'vocab'))  74.4 us
    psum x1, blocking collectives, shards(): lax.psum((jnp.sum(jnp.exp(teacher_logits - teacher_top[:, None]), axis=1)...  72.9 us
    all_gather x1, waiting for transfers between devices, shards(): student_full = lax.all_gather(student_wide, 'dp', axis=0, tiled=True)  62.4 us
    psum x1, blocking collectives, shards(): lax.psum(jnp.sum(normed_grad * scaled_own, axis=0), 'dp')  54.7 us
  transfers between devices with their start and end apart: 5, of which 5 were waited for; matrix products, arithmetic and copies ran while one was open for 1% of the time, Pallas kernels for 0%

commit v1 on v0

v1 whole, which is shorter than its diff:
```python
import functools
import math

import jax
import jax.numpy as jnp
from jax import lax
from jax.experimental import pallas as pl
from jax.experimental.pallas import tpu as pltpu
from jax.sharding import PartitionSpec as P

EPSILON = 1e-05
MIX_WEIGHT = 0.3
NLL_WEIGHT = 0.03
LOSS_SCALE = 8192.0
MESH = pl.DeviceIdType.MESH
F32 = jnp.float32
BF16 = jnp.bfloat16
X, Y, Z = 4, 4, 8
TOKENS, DT, DS, WIDTH = 256, 16384, 8192, 256


def kernel(
    t_rows, t_gain, t_head, s_rows, s_gain, s_head, ids, mask,
    loss_out, grad_out, gain_out,
    g0, g1, g2, t_w, s_w, t_inv, s_inv, t_acc, s_acc, dot_col, lg,
    sib_out, sib_in, ra, rb, ra_in1, rb_in1, ra2, rb2, ra_in2, rb_in2, ra3, rb3, ra_in3, rb_in3,
    st_c, st_x, st_y, st_z, gg_c, gg_x, gg_z,
    head_sem, ab_send, ab_recv, ring_send, ring_recv, core_send, core_recv,
    st_send, st_recv, sib_send_sem, sib_recv_sem, rs_send, rs_recv, gg_send, gg_recv,
):
    dp = lax.axis_index("dp")
    vo = lax.axis_index("vocab")
    c = lax.rem(dp, 2)
    x = lax.rem(lax.div(dp, 2), X)
    zl = lax.div(dp, 2 * X)
    y = lax.div(vo, 2)
    zh = lax.rem(vo, 2)
    z = zh * 4 + zl

    def device(x_, y_, z_, c_):
        return ((lax.rem(z_, 4) * X + x_) * 2 + c_, y_ * 2 + lax.div(z_, 4))

    to_c = lambda j: (dp - c + j, vo)
    to_x = lambda j: (dp + (j - x) * 2, vo)
    to_y = lambda j: (dp, vo + (j - y) * 2)
    to_z = lambda j: device(x, y, j, c)
    to_zl = lambda j: (dp + (j - zl) * 2 * X, vo)
    axis_c, axis_x, axis_y, axis_z = (2, c, to_c), (X, x, to_x), (Y, y, to_y), (Z, z, to_z)

    def remote(src, dst, send, recv, to):
        return pltpu.make_async_remote_copy(
            src_ref=src, dst_ref=dst, send_sem=send, recv_sem=recv, device_id=to, device_id_type=MESH
        )

    t_load = pltpu.make_async_copy(t_head, t_w, head_sem.at[0])
    s_load = pltpu.make_async_copy(s_head, s_w, head_sem.at[1])
    t_load.start()
    s_load.start()

    g0[c, z, y, x] = t_rows[0:16, :]
    g1[c, x, y, z] = t_rows[16:32, :]
    own_rows = s_rows[...].astype(F32)
    g2[c, y, x, z] = jnp.concatenate([own_rows[:, :512], own_rows[:, 512:]], axis=0).astype(BF16)

    def lane_sums(block):
        total = block[:, 0:128]
        for k in range(1, block.shape[1] // 128):
            total = total + block[:, k * 128 : (k + 1) * 128]
        total = jnp.concatenate([total] * (TOKENS // total.shape[0]), axis=0)
        return jnp.sum(total.T, axis=0, keepdims=True)

    lanes = lax.broadcasted_iota(jnp.int32, (1, TOKENS), 1)
    t_own = t_rows[...].astype(F32)
    t_squares = jnp.where(lax.div(lanes, 32) == vo, lane_sums(t_own * t_own), 0.0)
    s_squares = jnp.where(lax.div(lanes, 8) == dp, lane_sums(own_rows * own_rows), 0.0)
    pad = lambda rows: jnp.concatenate(rows + [jnp.zeros((8 - len(rows), TOKENS), F32)], axis=0)

    barrier = pltpu.get_barrier_semaphore()
    partners = 0
    for n, me, to in (axis_c, axis_x, axis_y, axis_z):
        for k in range(1, n):
            pl.semaphore_signal(barrier, inc=1, device_id=to(lax.rem(me + k, n)), device_id_type=MESH)
            partners += 1
    pl.semaphore_wait(barrier, partners)

    def all_partners(n, me, to, src, dst, send, recv):
        copies = []
        for k in range(1, n):
            j = lax.rem(me + k, n)
            copy = remote(src(j), dst(me), send(k), recv(me), to(j))
            copy.start()
            copies.append((copy, remote(dst(j), dst(j), send(k), recv(j), to(j))))

        def wait():
            for copy, arrival in copies:
                arrival.wait_recv()
            for copy, arrival in copies:
                copy.wait_send()

        return wait

    def exchange(r, value, combine, result):
        base = 0
        for (n, me, to), buf in zip((axis_c, axis_x, axis_y, axis_z), (st_c, st_x, st_y, st_z)):
            buf[r, me] = value
            wait = all_partners(
                n, me, to,
                lambda j: buf.at[r, me],
                lambda j: buf.at[r, j],
                lambda k: st_send.at[r, base + k],
                lambda j: st_recv.at[r, base + j],
            )
            yield
            wait()
            value = combine([buf[r, j] for j in range(n)])
            base += n
        result.append(value)

    def finish(steps):
        for _ in steps:
            pass

    def add_all(values):
        return functools.reduce(lambda a, b: a + b, values)

    parts = (
        (g0, (axis_x, axis_y, axis_z)),
        (g1, (axis_z, axis_y, axis_x)),
        (g2, (axis_z, axis_x, axis_y)),
    )
    waits = []
    for p, (g, ((na, a, to_a), (_, b, _), (_, cc, _))) in enumerate(parts):
        waits.append(
            all_partners(
                na, a, to_a,
                lambda j: g.at[c, cc, b, a],
                lambda j: g.at[c, cc, b, j],
                lambda k: ab_send.at[p, 0, k],
                lambda j: ab_recv.at[p, 0, j],
            )
        )
    squares = []
    round0 = exchange(0, pad([t_squares, s_squares]), add_all, squares)
    next(round0)
    next_waits = []
    for p, (g, (_, (nb, b, to_b), (_, cc, _))) in enumerate(parts):
        waits[p]()
        next_waits.append(
            all_partners(
                nb, b, to_b,
                lambda j: g.at[c, cc, b],
                lambda j: g.at[c, cc, j],
                lambda k: ab_send.at[p, 1, k],
                lambda j: ab_recv.at[p, 1, j],
            )
        )
    next(round0)

    class Ring:
        def __init__(self, p, g, n, me, to):
            self.p, self.g, self.n, self.me = p, g, n, me
            self.to = (to(lax.rem(me + 1, n)), to(lax.rem(me + n - 1, n)))
            self.sent, self.forwarded = [], []

        def piece(self, way, i, distance, core):
            half = i % 2 if way == 0 else 1 - i % 2
            plane = lax.rem(self.me + (self.n - distance if way == 0 else distance), self.n)
            return self.g.at[core, plane, 2 * half : 2 * half + 2]

        def send(self, way, i):
            ref = self.piece(way, i, i // 2, c)
            copy = remote(ref, ref, ring_send.at[self.p, way, i], ring_recv.at[self.p, way, i], self.to[way])
            copy.start()
            self.sent.append(copy)

        def forward(self, mine, theirs, k):
            copy = remote(mine, mine, core_send.at[self.p, k], core_recv.at[self.p, k], to_c(1 - c))
            copy.start()
            self.forwarded.append((copy, remote(theirs, theirs, core_send.at[self.p, k], core_recv.at[self.p, k], to_c(1 - c))))

        def begin(self):
            for i in range(2):
                for way in range(2):
                    self.send(way, i)
            self.forward(self.g.at[c, self.me], self.g.at[1 - c, self.me], 0)

        def event(self, i):
            for way in range(2):
                ref = self.piece(way, i, i // 2 + 1, c)
                remote(ref, ref, ring_send.at[self.p, way, i], ring_recv.at[self.p, way, i], self.to[way]).wait_recv()
                if i + 2 <= self.n - 2:
                    self.send(way, i + 2)
                self.forward(ref, self.piece(way, i, i // 2 + 1, 1 - c), 1 + 2 * i + way)

        def end(self):
            for copy in self.sent:
                copy.wait_send()
            for copy, arrival in self.forwarded:
                arrival.wait_recv()
                copy.wait_send()

    rings = []
    for p, (g, (_, _, (n, me, to))) in enumerate(parts):
        next_waits[p]()
        ring = Ring(p, g, n, me, to)
        ring.begin()
        rings.append(ring)
    next(round0)
    rings[0].event(0)
    next(round0)
    rings[0].event(1)
    finish(round0)
    squares = squares[0]
    t_inv_row = lax.rsqrt(squares[0:1] / DT + EPSILON)
    s_inv_row = lax.rsqrt(squares[1:2] / DS + EPSILON)
    column = lambda row: jnp.broadcast_to(row, (128, TOKENS)).T
    t_inv[...] = column(t_inv_row)
    s_inv[...] = column(s_inv_row)
    rings[1].event(0)
    rings[2].event(0)
    rings[0].event(2)
    rings[0].event(3)
    rings[1].event(1)
    rings[2].event(1)
    rings[0].event(4)
    rings[0].event(5)
    rings[1].event(2)
    rings[2].event(2)
    rings[0].event(6)
    t_load.wait()
    s_load.wait()
    wide = lambda block: jnp.concatenate([block] * 4, axis=1)

    rings[2].end()
    s_acc[...] = jnp.zeros_like(s_acc)

    def student_step(v, carry):
        y_, zh_ = lax.div(v, 2), lax.rem(v, 2)
        gains = [s_gain[pl.ds(v * 2 + h, 1), :] for h in range(2)]
        blocks = ([], [])
        for pair in range(16):
            scaled = []
            for core in range(2):
                d = pair * 2 + core
                raw = g2[core, y_, pair % 4, zh_ * 4 + pair // 4].astype(F32)
                inv = wide(s_inv[d * 8 : d * 8 + 8, :])
                scaled.append((raw[0:8] * inv, raw[8:16] * inv))
            for h in range(2):
                both = jnp.concatenate([scaled[0][h], scaled[1][h]], axis=0) * gains[h]
                blocks[h].append(both.astype(BF16))
        total = s_acc[...]
        for h in range(2):
            w = s_w[pl.ds(pl.multiple_of(v * 1024 + h * 512, 512), 512), :]
            total += jnp.dot(jnp.concatenate(blocks[h], axis=0), w, preferred_element_type=F32)
        s_acc[...] = total
        return carry

    lax.fori_loop(0, 8, student_step, 0)

    rings[0].end()
    rings[1].end()
    t_acc[...] = jnp.zeros_like(t_acc)

    def teacher_step(d, carry):
        c_, x_, zl_ = lax.rem(d, 2), lax.rem(lax.div(d, 2), X), lax.div(d, 2 * X)
        gain = t_gain[pl.ds(d, 1), :]
        blocks = []
        for v in range(8):
            for p in range(2):
                z_ = (v % 2) * 4 + zl_
                raw = g0[c_, z_, v // 2, x_] if p == 0 else g1[c_, x_, v // 2, z_]
                inv = wide(t_inv[v * 32 + p * 16 : v * 32 + p * 16 + 16, :])
                blocks.append((raw.astype(F32) * inv * gain).astype(BF16))
        w = t_w[pl.ds(pl.multiple_of(d * 512, 512), 512), :]
        t_acc[...] += jnp.dot(jnp.concatenate(blocks, axis=0), w, preferred_element_type=F32)
        return carry

    lax.fori_loop(0, 32, teacher_step, 0)

    t_acc[...] = t_acc[...].T
    s_acc[...] = s_acc[...].T
    tl, sl = t_acc[...], s_acc[...]
    column_start = (dp * 8 + vo) * WIDTH
    onehot = (column_start + lax.broadcasted_iota(jnp.int32, (WIDTH, TOKENS), 0) == ids[...]).astype(F32)
    t_top = jnp.max(tl, axis=0, keepdims=True)
    s_top = jnp.max(sl, axis=0, keepdims=True)
    over_v = lambda a: jnp.sum(a, axis=0, keepdims=True)

    def merge(values):
        rows = []
        for k in (0, 2):
            top = functools.reduce(jnp.maximum, [v[k : k + 1] for v in values])
            rows += [top, add_all([v[k + 1 : k + 2] * jnp.exp(v[k : k + 1] - top) for v in values])]
        return pad(rows + [add_all([v[4:5] for v in values])])

    first = []
    finish(
        exchange(
            1,
            pad([t_top, over_v(jnp.exp(tl - t_top)), s_top, over_v(jnp.exp(sl - s_top)), over_v(onehot * sl)]),
            merge,
            first,
        )
    )
    first = first[0]
    t_lse = first[0:1] + jnp.log(first[1:2])
    s_lse = first[2:3] + jnp.log(first[3:4])
    picked = first[4:5]
    t_logp = t_acc[...] - t_lse
    s_logp = s_acc[...] - s_lse
    a, b = math.log(MIX_WEIGHT) + t_logp, math.log(1.0 - MIX_WEIGHT) + s_logp
    mix_logp = jnp.maximum(a, b) + jnp.log1p(jnp.exp(-jnp.abs(a - b)))
    p_, q = jnp.exp(t_logp), jnp.exp(s_logp)
    gap = s_logp - mix_logp
    q_gap = q * gap
    jsd_part = over_v(MIX_WEIGHT * p_ * (t_logp - mix_logp) + (1.0 - MIX_WEIGHT) * q_gap)
    second = []
    finish(
        exchange(
            2,
            pad([jsd_part, over_v(q_gap), over_v(q_gap * s_logp), over_v(q * s_logp)]),
            add_all,
            second,
        )
    )
    second = second[0]
    jsd, kl = second[0:1], second[1:2]
    weights = mask[...].astype(F32)
    count = jnp.sum(weights, axis=1, keepdims=True)
    loss = jnp.sum(weights * (jsd + NLL_WEIGHT * (s_lse - picked)), axis=1, keepdims=True) / count
    loss_out[...] = jnp.broadcast_to(loss, loss_out.shape)
    row_scale = LOSS_SCALE * weights / count
    rest = 1.0 - MIX_WEIGHT
    row_dot = row_scale * (
        rest * (second[2:3] - kl * second[3:4]) + NLL_WEIGHT * (second[3:4] - (picked - s_lse))
    ) / DS
    dot_col[...] = column(row_dot)
    logit_grad = row_scale * (q * (rest * gap - rest * kl) + NLL_WEIGHT * (q - onehot))
    lg[...] = logit_grad.T.reshape(16, 2, 8, WIDTH)
    lhs = jnp.concatenate([lg[:, 1 - c].reshape(128, WIDTH), lg[:, c].reshape(128, WIDTH)], axis=0).astype(BF16)

    sibling = to_c(1 - c)

    def sib_copy(v):
        return remote(sib_out.at[v], sib_in.at[v], sib_send_sem.at[v], sib_recv_sem.at[v], sibling)

    def grad_step(v, carry):
        y_, zh_ = lax.div(v, 2), lax.rem(v, 2)
        halves = []
        for h in range(2):
            w = s_w[pl.ds(pl.multiple_of(v * 1024 + h * 512, 512), 512), :]
            halves.append(
                lax.dot_general(lhs, w, (((1,), (1,)), ((), ())), preferred_element_type=F32).reshape(2, 16, 8, 512)
            )
        both = jnp.concatenate(halves, axis=2).astype(BF16)
        sib_out[v] = both[0]
        sib_copy(v).start()
        for i in range(16):
            ra[i % 4, y_, zh_ * 4 + i // 4] = both[1, i, :, :256]
            rb[y_, i % 4, zh_ * 4 + i // 4] = both[1, i, :, 256:]
        return carry

    lax.fori_loop(0, 8, grad_step, 0)

    def sib_step(v, carry):
        y_, zh_ = lax.div(v, 2), lax.rem(v, 2)
        sib_copy(v).wait()
        for i in range(16):
            got = sib_in[v, i].astype(F32)
            at_a = (i % 4, y_, zh_ * 4 + i // 4)
            at_b = (y_, i % 4, zh_ * 4 + i // 4)
            ra[at_a] = (ra[at_a].astype(F32) + got[:, :256]).astype(BF16)
            rb[at_b] = (rb[at_b].astype(F32) + got[:, 256:]).astype(BF16)
        return carry

    lax.fori_loop(0, 8, sib_step, 0)

    def scatter(axis, src, landing, part, phase):
        n, me, to = axis
        return all_partners(
            n, me, to,
            lambda j: src.at[j],
            lambda j: landing.at[j],
            lambda k: rs_send.at[part, phase, k],
            lambda j: rs_recv.at[part, phase, j],
        )

    def add_up(axis, src, landing, out):
        n, me, _ = axis

        def total(at):
            value = src[(me,) + at].astype(F32)
            for k in range(1, n):
                value = value + landing[(lax.rem(me + k, n),) + at].astype(F32)
            return value

        if out is None:
            return total(())
        lead = out.shape[:-2]

        def step(i, carry):
            for j in range(lead[-1]):
                at = (i, j) if len(lead) == 2 else (j,)
                out[at] = total(at).astype(BF16)
            return carry

        if len(lead) == 2:
            lax.fori_loop(0, lead[0], step, 0)
        else:
            step(0, 0)

    wait_a = scatter(axis_x, ra, ra_in1, 0, 0)
    wait_b = scatter(axis_y, rb, rb_in1, 1, 0)
    wait_a()
    add_up(axis_x, ra, ra_in1, ra2)
    wait_a = scatter(axis_y, ra2, ra_in2, 0, 1)
    wait_b()
    add_up(axis_y, rb, rb_in1, rb2)
    wait_b = scatter(axis_x, rb2, rb_in2, 1, 1)
    wait_a()
    add_up(axis_y, ra2, ra_in2, ra3)
    wait_a = scatter(axis_z, ra3, ra_in3, 0, 2)
    wait_b()
    add_up(axis_x, rb2, rb_in2, rb3)
    wait_b = scatter(axis_z, rb3, rb_in3, 1, 2)
    wait_a()
    total_a = add_up(axis_z, ra3, ra_in3, None)
    wait_b()
    total_b = add_up(axis_z, rb3, rb_in3, None)
    normed_grad = jnp.concatenate([total_a, total_b], axis=1)

    own = pl.ds(pl.multiple_of(dp * 8, 8), 8)
    inv = wide(s_inv[own, :])
    dots = wide(dot_col[own, :])
    pieces = []
    for h in range(2):
        grad = normed_grad[h * 8 : h * 8 + 8]
        scaled = own_rows[:, h * 512 : (h + 1) * 512] * inv
        gain = s_gain[pl.ds(vo * 2 + h, 1), :]
        grad_out[:, h * 512 : (h + 1) * 512] = inv * (grad * gain - scaled * dots)
        row = jnp.sum(grad * scaled, axis=0, keepdims=True)
        pieces += [row[:, k * 128 : (k + 1) * 128] for k in range(4)]
    value = jnp.concatenate(pieces, axis=0)
    base = 0
    for (n, me, to), buf in ((axis_c, gg_c), (axis_x, gg_x), ((4, zl, to_zl), gg_z)):
        buf[me] = value
        all_partners(
            n, me, to,
            lambda j: buf.at[me],
            lambda j: buf.at[j],
            lambda k: gg_send.at[base + k],
            lambda j: gg_recv.at[base + j],
        )()
        value = add_all([buf[j] for j in range(n)])
        base += n
    gain_out[...] = value


def shards(t_rows, t_gain, t_head, s_rows, s_gain, s_head, ids, mask):
    vmem = pl.BlockSpec(memory_space=pltpu.VMEM)
    hbm = pl.BlockSpec(memory_space=pl.ANY)
    dma = pltpu.SemaphoreType.DMA
    scratch = [
        pltpu.VMEM((2, Z, Y, X, 16, 512), BF16),
        pltpu.VMEM((2, X, Y, Z, 16, 512), BF16),
        pltpu.VMEM((2, Y, X, Z, 16, 512), BF16),
        pltpu.VMEM((DT, WIDTH), BF16),
        pltpu.VMEM((DS, WIDTH), BF16),
        pltpu.VMEM((TOKENS, 128), F32),
        pltpu.VMEM((TOKENS, 128), F32),
        pltpu.VMEM((TOKENS, WIDTH), F32),
        pltpu.VMEM((TOKENS, WIDTH), F32),
        pltpu.VMEM((TOKENS, 128), F32),
        pltpu.VMEM((16, 2, 8, WIDTH), F32),
        pltpu.VMEM((8, 16, 16, 512), BF16),
        pltpu.VMEM((8, 16, 16, 512), BF16),
        pltpu.VMEM((X, Y, Z, 16, 256), BF16),
        pltpu.VMEM((Y, X, Z, 16, 256), BF16),
        pltpu.VMEM((X, Y, Z, 16, 256), BF16),
        pltpu.VMEM((Y, X, Z, 16, 256), BF16),
        pltpu.VMEM((Y, Z, 16, 256), BF16),
        pltpu.VMEM((X, Z, 16, 256), BF16),
        pltpu.VMEM((Y, Z, 16, 256), BF16),
        pltpu.VMEM((X, Z, 16, 256), BF16),
        pltpu.VMEM((Z, 16, 256), BF16),
        pltpu.VMEM((Z, 16, 256), BF16),
        pltpu.VMEM((Z, 16, 256), BF16),
        pltpu.VMEM((Z, 16, 256), BF16),
        pltpu.VMEM((3, 2, 8, TOKENS), F32),
        pltpu.VMEM((3, X, 8, TOKENS), F32),
        pltpu.VMEM((3, Y, 8, TOKENS), F32),
        pltpu.VMEM((3, Z, 8, TOKENS), F32),
        pltpu.VMEM((2, 8, 128), F32),
        pltpu.VMEM((X, 8, 128), F32),
        pltpu.VMEM((4, 8, 128), F32),
        dma((2,)),
        dma((3, 2, 8)),
        dma((3, 2, 8)),
        dma((3, 2, 7)),
        dma((3, 2, 7)),
        dma((3, 15)),
        dma((3, 15)),
        dma((3, 18)),
        dma((3, 18)),
        dma((8,)),
        dma((8,)),
        dma((2, 3, 8)),
        dma((2, 3, 8)),
        dma((10,)),
        dma((10,)),
    ]
    flops = 2 * TOKENS * WIDTH * (DT + 2 * DS)
    loss, grad, gain = pl.pallas_call(
        kernel,
        out_shape=(
            jax.ShapeDtypeStruct((8, 128), F32),
            jax.ShapeDtypeStruct(s_rows.shape, F32),
            jax.ShapeDtypeStruct((8, 128), F32),
        ),
        in_specs=[vmem, vmem, hbm, vmem, vmem, hbm, vmem, vmem],
        out_specs=(vmem, vmem, vmem),
        scratch_shapes=scratch,
        compiler_params=pltpu.CompilerParams(
            collective_id=0, has_side_effects=True, vmem_limit_bytes=56 * 1024 * 1024
        ),
        cost_estimate=pl.CostEstimate(flops=flops, bytes_accessed=2 * WIDTH * (DT + DS), transcendentals=0),
    )(
        t_rows,
        t_gain.astype(F32).reshape(DT // 512, 512),
        t_head,
        s_rows,
        s_gain.astype(F32).reshape(DS // 512, 512),
        s_head,
        ids.reshape(1, TOKENS),
        mask.reshape(1, TOKENS),
    )
    return loss[0, 0], grad.astype(BF16), gain.reshape(1024)


def solution(mesh):
    return jax.shard_map(
        shards,
        mesh=mesh,
        in_specs=(
            P("vocab", "dp"),
            P(),
            P(None, ("dp", "vocab")),
            P("dp", "vocab"),
            P(),
            P(None, ("dp", "vocab")),
            P(),
            P(),
        ),
        out_specs=(P(), P("dp", "vocab"), P("vocab")),
        check_vma=False,
    )
```

time: 897 us -> 141 us (0.16); the launches traced: 881 us -> 139 us
  waiting for transfers between devices: 477 us -> 0 us
  blocking collectives: 351 us -> 0 us
  Pallas kernels: 0 us -> 131 us
  matrix products: 22.3 us -> 0 us
  between operations: 16.3 us -> 0.64 us
  other arithmetic: 14.6 us -> 1.36 us
    all_gather x3 -> x0, waiting for transfers between devices: 243 us -> none  [the longest x1 165 us: shards(): teacher_full = lax.all_gather(teacher_wide, 'vocab', axis=0, tiled=True)]
    reduce_scatter x2 -> x0, waiting for transfers between devices: 233 us -> none  [the longest x1 131 us: shards(): lax.psum_scatter(lax.dot_general(logit_grad, student_head, (((1,), (1,)),...]
    psum x4 -> x0, blocking collectives: 228 us -> none  [the longest x1 74.4 us: shards(): jsd, kl_student = lax.psum((jsd_part, kl_part), ('dp', 'vocab'))]
    pallas_call x0 -> x1, Pallas kernels: none -> 131 us  [shards(): pl.pallas_call(kernel, out_shape=(jax.ShapeDtypeStruct((8, 128), F32), ja...]
    pmax x1 -> x0, blocking collectives: 75.9 us -> none  [shards(): lax.pmax((teacher_local_top, student_local_top), ('dp', 'vocab'))]
    all_gather x1 -> x0, blocking collectives: 47 us -> none  [shards(): student_wide = lax.all_gather(student_rows, 'vocab', axis=1, tiled=True)]
    dot_general x3 -> x0, matrix products: 22.3 us -> none  [the longest x1 9.75 us: shards(): jnp.dot(teacher_normed, teacher_head, preferred_element_type=jnp.float32)]
    reduce_sum x6 -> x0, other arithmetic: 10.3 us -> none  [the longest x2 8.24 us: rms_inverse(): jnp.mean(widened * widened, axis=1, keepdims=True) + EPSILON]
  transfers between devices with their start and end apart: 5 -> 0, of which waited for: 5 -> 0; matrix products, arithmetic and copies ran while one was open for 1% -> 0% of each run, Pallas kernels for 0% -> 0%
where the time goes in v1:
time: 141 us; the launch traced here: 139 us
  Pallas kernels  131 us (93%)
  local copies, waits for them, and re-layouts  5.21 us (4%)
    pallas_call x1, Pallas kernels, shards(): pl.pallas_call(kernel, out_shape=(jax.ShapeDtypeStruct((8, 128), F32), ja...  131 us

profile of v1, /device:TPU:32, one launch (start us, length us, event | category | flops | bytes accessed | tf_op | source)
XLA Modules:
  0.0 138.7 jit_solution(1023221533743560692)
XLA Ops:
  0.6 1.3 reshape.35.s_gain
  2.0 1.4 %reshape.33.t_gain = f32[32,512]{1,0:T(8,128)} reshape(bf16[16384]{0:T(1024)(128)(2,1)} %param.9) | data formatting | bytes 98304 | tf_op jit(solution)/shard_map/reshape | solution.py:529
  3.4 131.5 %shard_map.103 = (f32[8,128]{1,0:T(8,128)}, f32[8,1024]{1,0:T(8,128)}, f32[8,128]{1,0:T(8,128)}) custom-call(bf16[32,512]{1,0:T(8,128)(2,1)} %t_rows.1, f32[32,512]{1,0:T(8,128)} %reshape.33.t_gain, bf16[16384,256]{1,0:T(8,128)(2,1)} %t_head.1, bf16[8,1024]{1,0:T(8,128)(2,1)} %s_rows.1, f32[16,512]{1,0:T(8,128)} %reshape.35.s_gain, ...), custom_call_target="tpu_custom_call" | custom-call | flops 4294967296 | bytes 12582912 | tf_op jit(solution)/shard_map/pallas_call | solution.py:513
  134.8 1.2 slice.3
  136.0 1.4 convert_element_type.2
  137.4 1.3 copy.12

commit v2 on v1

v2 whole, which is shorter than its diff:
```python
import functools
import math

import jax
import jax.numpy as jnp
from jax import lax
from jax.experimental import pallas as pl
from jax.experimental.pallas import tpu as pltpu
from jax.sharding import PartitionSpec as P

EPSILON = 1e-05
MIX_WEIGHT = 0.3
NLL_WEIGHT = 0.03
LOSS_SCALE = 8192.0
MESH = pl.DeviceIdType.MESH
F32 = jnp.float32
BF16 = jnp.bfloat16
X, Y, Z = 4, 4, 8
TOKENS, DT, DS, WIDTH = 256, 16384, 8192, 256


def kernel(
    t_rows, t_gain_in, t_head, s_rows, s_gain_in, s_head, ids, mask,
    loss_out, grad_out, gain_out,
    g0, g1, g2, t_w, s_w, t_gain, s_gain, t_inv, s_inv, t_acc0, t_acc1, t_acc, s_acc, dot_col, lg,
    sib_out, sib_in, raf, rbf, ra_out, rb_out, ra_via, rb_via, ra_in, rb_in,
    raf2, rbf2, ra2, rb2, ra_in2, rb_in2, raf3, rbf3, ra3, rb3, ra_in3, rb_in3,
    st_c, st_p, st_z, gp_c, gp1, gp_y, gp_x, gp3, gp_z,
    head_sem, a_send, a_recv, b_send, b_recv, ring_send, ring_recv, core_send, core_recv,
    st_send, st_recv, sib_send_sem, sib_recv_sem, first_send, first_recv, rs_send, rs_recv, gp_send, gp_recv,
):
    dp = lax.axis_index("dp")
    vo = lax.axis_index("vocab")
    c = lax.rem(dp, 2)
    x = lax.rem(lax.div(dp, 2), X)
    zl = lax.div(dp, 2 * X)
    y = lax.div(vo, 2)
    zh = lax.rem(vo, 2)
    z = zh * 4 + zl

    def device(x_, y_, z_, c_):
        return ((lax.rem(z_, 4) * X + x_) * 2 + c_, y_ * 2 + lax.div(z_, 4))

    to_c = lambda j: (dp - c + j, vo)
    to_x = lambda j: (dp + (j - x) * 2, vo)
    to_y = lambda j: (dp, vo + (j - y) * 2)
    to_z = lambda j: device(x, y, j, c)
    to_p = lambda j: device(lax.div(j, Y), lax.rem(j, Y), z, c)
    axis_c, axis_x, axis_y, axis_z = (2, c, to_c), (X, x, to_x), (Y, y, to_y), (Z, z, to_z)
    axis_p = (X * Y, x * Y + y, to_p)

    barrier = pltpu.get_barrier_semaphore()
    partners = 0
    for n, me, to in (axis_z, axis_p, axis_c):
        for k in range(1, n):
            pl.semaphore_signal(barrier, inc=1, device_id=to(lax.rem(me + k, n)), device_id_type=MESH)
            partners += 1

    def remote(src, dst, send, recv, to):
        return pltpu.make_async_remote_copy(
            src_ref=src, dst_ref=dst, send_sem=send, recv_sem=recv, device_id=to, device_id_type=MESH
        )

    late = []

    def start(src, dst, send, recv, to):
        copy = remote(src, dst, send, recv, to)
        copy.start()
        late.append(copy)

    def arrived(dst, send, recv, to):
        remote(dst, dst, send, recv, to).wait_recv()

    p0 = x * Y + y
    g0[c, z, p0] = t_rows[0:16, :]
    g1[c, x, y, z] = t_rows[16:32, :]
    own_rows = s_rows[...].astype(F32)
    g2[c, y, x, z] = jnp.concatenate([own_rows[:, :512], own_rows[:, 512:]], axis=0).astype(BF16)

    def lane_sums(block):
        total = block[:, 0:128]
        for k in range(1, block.shape[1] // 128):
            total = total + block[:, k * 128 : (k + 1) * 128]
        total = jnp.concatenate([total] * (TOKENS // total.shape[0]), axis=0)
        return jnp.sum(total.T, axis=0, keepdims=True)

    lanes = lax.broadcasted_iota(jnp.int32, (1, TOKENS), 1)
    t_own = t_rows[...].astype(F32)
    t_squares = jnp.where(lax.div(lanes, 32) == vo, lane_sums(t_own * t_own), 0.0)
    s_squares = jnp.where(lax.div(lanes, 8) == dp, lane_sums(own_rows * own_rows), 0.0)
    pad = lambda rows: jnp.concatenate(rows + [jnp.zeros((8 - len(rows), TOKENS), F32)], axis=0)
    squares_value = pad([t_squares, s_squares])

    pl.semaphore_wait(barrier, partners)

    def all_partners(axis, src, dst, send, recv):
        n, me, to = axis
        arrivals = []
        for k in range(1, n):
            j = lax.rem(me + k, n)
            start(src(j), dst(me), send(k), recv(me), to(j))
            arrivals.append(remote(dst(j), dst(j), send(k), recv(j), to(j)))

        def wait():
            for arrival in arrivals:
                arrival.wait_recv()

        return wait

    def exchange(r, value, combine, result):
        base = 0
        for axis, buf in ((axis_c, st_c), (axis_p, st_p), (axis_z, st_z)):
            n, me, _ = axis
            buf[r, me] = value
            wait = all_partners(
                axis,
                lambda j: buf.at[r, me],
                lambda j: buf.at[r, j],
                lambda k: st_send.at[r, base + k],
                lambda j: st_recv.at[r, base + j],
            )
            yield
            wait()
            value = combine([buf[r, j] for j in range(n)])
            base += n
        result.append(value)

    def finish(steps):
        for _ in steps:
            pass

    def add_all(values):
        return functools.reduce(lambda a, b: a + b, values)

    class Rows:
        def __init__(self, p, g, a, b, cc):
            self.p, self.g, self.a, self.b, self.c = p, g, a, b, cc
            step = lambda axis: tuple(axis[2](lax.rem(axis[1] + k, 4)) for k in (1, 3))
            self.to_b, self.to_c = step(b), step(cc)
            self.ready = set()

        def begin(self):
            mine, theirs = self.c[1], self.b[1]
            self.wait_a = all_partners(
                self.a,
                lambda j: self.g.at[c, mine, theirs, self.a[1]],
                lambda j: self.g.at[c, mine, theirs, j],
                lambda k: a_send.at[self.p, k],
                lambda j: a_recv.at[self.p, j],
            )

        def row(self, core, plane, r):
            return self.g.at[core, lax.rem(self.c[1] + plane, 4), lax.rem(self.b[1] + r, 4)]

        def cross(self, plane, r):
            k = plane * 4 + r
            ref = self.row(c, plane, r)
            start(ref, ref, core_send.at[self.p, k], core_recv.at[self.p, k], to_c(1 - c))

        def crossed(self, plane):
            for r in range(4):
                k = plane * 4 + r
                arrived(self.row(1 - c, plane, r), core_send.at[self.p, k], core_recv.at[self.p, k], to_c(1 - c))

        def half(self, r, way):
            return self.row(c, 0, r).at[4 * way : 4 * way + 4]

        def send_b(self, way, item):
            ref = self.row(c, 0, 0) if item == 0 else self.half(3 if way == 0 else 1, way)
            start(ref, ref, b_send.at[self.p, way, item], b_recv.at[self.p, way, item], self.to_b[way])

        def take_b(self, item):
            for way in range(2):
                ref = self.row(c, 0, 3 if way == 0 else 1) if item == 0 else self.half(2, way)
                arrived(ref, b_send.at[self.p, way, item], b_recv.at[self.p, way, item], self.to_b[way])
                if item == 0:
                    self.send_b(way, 1)
            if item == 0:
                self.send_c(0, 1)
                self.send_c(1, 3)
                self.cross(0, 1)
                self.cross(0, 3)
            else:
                self.send_c(0, 2)
                self.send_c(1, 2)
                self.cross(0, 2)

        def send_c(self, way, r, hop=0):
            ref = self.row(c, 0 if hop == 0 else (3 if way == 0 else 1), r)
            k = r + 4 * hop
            start(ref, ref, ring_send.at[self.p, way, k], ring_recv.at[self.p, way, k], self.to_c[way])

        def take_c(self, way, r, hop=0):
            plane = 2 if hop else (3 if way == 0 else 1)
            k = r + 4 * hop
            arrived(self.row(c, plane, r), ring_send.at[self.p, way, k], ring_recv.at[self.p, way, k], self.to_c[way])
            if hop == 0 and r in ((0, 1), (3, 2))[way]:
                self.send_c(way, r, 1)
            self.cross(plane, r)

        def after_a(self):
            self.wait_a()
            for way in range(2):
                self.send_b(way, 0)
                self.send_c(way, 0)
            self.cross(0, 0)

    class Ring:
        def __init__(self, g, n, me, to):
            self.g, self.n, self.me = g, n, me
            self.to = (to(lax.rem(me + 1, n)), to(lax.rem(me + n - 1, n)))

        def piece(self, way, i, distance, core):
            half = i % 2 if way == 0 else 1 - i % 2
            plane = lax.rem(self.me + (self.n - distance if way == 0 else distance), self.n)
            return self.g.at[core, plane, 8 * half : 8 * half + 8]

        def send(self, way, i):
            ref = self.piece(way, i, i // 2, c)
            start(ref, ref, ring_send.at[0, way, i], ring_recv.at[0, way, i], self.to[way])

        def begin(self):
            for i in range(2):
                for way in range(2):
                    self.send(way, i)
            ref = self.g.at[c, self.me]
            start(ref, ref, core_send.at[0, 0], core_recv.at[0, 0], to_c(1 - c))

        def event(self, i):
            for way in range(2):
                ref = self.piece(way, i, i // 2 + 1, c)
                arrived(ref, ring_send.at[0, way, i], ring_recv.at[0, way, i], self.to[way])
                if i + 2 <= self.n - 2:
                    self.send(way, i + 2)
                k = 1 + 2 * i + way
                start(ref, ref, core_send.at[0, k], core_recv.at[0, k], to_c(1 - c))

        def crossed(self, i):
            for way in range(2):
                k = 1 + 2 * i + way
                arrived(self.piece(way, i, i // 2 + 1, 1 - c), core_send.at[0, k], core_recv.at[0, k], to_c(1 - c))

        def crossed_own(self):
            arrived(self.g.at[1 - c, self.me], core_send.at[0, 0], core_recv.at[0, 0], to_c(1 - c))

    part1 = Rows(1, g1, axis_z, axis_y, axis_x)
    part2 = Rows(2, g2, axis_z, axis_x, axis_y)
    part0 = Ring(g0, Z, z, to_z)
    both = (part1, part2)

    wide = lambda block: jnp.concatenate([block] * 4, axis=1)

    def student_planes(count, plane_of):
        def step(i, carry):
            y_, zh_ = plane_of(lax.div(i, 2)), lax.rem(i, 2)
            v = y_ * 2 + zh_
            gains = [s_gain[pl.ds(v * 2 + h, 1), :] for h in range(2)]
            blocks = ([], [])
            for pair in range(16):
                scaled = []
                for core in range(2):
                    raw = g2[core, y_, pair % 4, zh_ * 4 + pair // 4].astype(F32)
                    inv = wide(s_inv[pair, core])
                    scaled.append((raw[0:8] * inv, raw[8:16] * inv))
                for h in range(2):
                    rows = jnp.concatenate([scaled[0][h], scaled[1][h]], axis=0) * gains[h]
                    blocks[h].append(rows.astype(BF16))
            total = s_acc[...]
            for h in range(2):
                w = s_w[pl.ds(pl.multiple_of(v * 1024 + h * 512, 512), 512), :]
                total += jnp.dot(jnp.concatenate(blocks[h], axis=0), w, preferred_element_type=F32)
            s_acc[...] = total
            return carry

        lax.fori_loop(0, 2 * count, step, 0)

    def teacher_step(acc, p, load, d):
        gain = t_gain[pl.ds(d, 1), :]
        blocks = []
        for v in range(8):
            inv = wide(t_inv[v * 32 + p * 16 : v * 32 + p * 16 + 16, :])
            blocks.append((load(v).astype(F32) * inv * gain).astype(BF16))
        w = t_w[pl.ds(pl.multiple_of(d * 512, 512), 512), :]
        acc[...] += jnp.dot(jnp.concatenate(blocks, axis=0), w, preferred_element_type=F32)

    def teacher_x(count, plane_of):
        def step(i, carry):
            x_, zl_, c_ = plane_of(lax.div(i, 8)), lax.div(lax.rem(i, 8), 2), lax.rem(i, 2)
            load = lambda v: g1[c_, x_, v // 2, (v % 2) * 4 + zl_]
            teacher_step(t_acc1, 1, load, (zl_ * X + x_) * 2 + c_)
            return carry

        lax.fori_loop(0, 8 * count, step, 0)

    def teacher_z(count, plane_of):
        def step(i, carry):
            zl_, x_, c_ = plane_of(lax.div(i, 8)), lax.div(lax.rem(i, 8), 2), lax.rem(i, 2)
            load = lambda v: g0[c_, (v % 2) * 4 + zl_, x_ * Y + v // 2]
            teacher_step(t_acc0, 0, load, (zl_ * X + x_) * 2 + c_)
            return carry

        lax.fori_loop(0, 8 * count, step, 0)

    for part in both:
        part.begin()
    wait_plane = all_partners(
        axis_p,
        lambda j: g0.at[c, z, p0],
        lambda j: g0.at[c, z, j],
        lambda k: a_send.at[0, k],
        lambda j: a_recv.at[0, j],
    )
    t_load = pltpu.make_async_copy(t_head, t_w, head_sem.at[0])
    s_load = pltpu.make_async_copy(s_head, s_w, head_sem.at[1])
    t_load.start()
    s_load.start()
    squares = []
    round0 = exchange(0, squares_value, add_all, squares)
    next(round0)
    t_gain[...] = t_gain_in[...].astype(F32).reshape(t_gain.shape)
    s_gain[...] = s_gain_in[...].astype(F32).reshape(s_gain.shape)
    for acc in (t_acc0, t_acc1, s_acc):
        acc[...] = jnp.zeros_like(acc)
    next(round0)
    for part in both:
        part.after_a()
    wait_plane()
    part0.begin()
    for part in both:
        part.take_b(0)
    for part in both:
        part.take_c(0, 0)
        part.take_c(1, 0)
        part.send_c(0, 3)
        part.send_c(1, 1)
    next(round0)
    part0.event(0)
    part0.event(1)
    for part in both:
        part.take_b(1)
    finish(round0)
    squares = squares[0]
    t_inv_row = lax.rsqrt(squares[0:1] / DT + EPSILON)
    s_inv_row = lax.rsqrt(squares[1:2] / DS + EPSILON)
    column = lambda row: jnp.broadcast_to(row, (128, TOKENS)).T
    t_inv[...] = column(t_inv_row)
    s_inv[...] = column(s_inv_row).reshape(s_inv.shape)
    for part in both:
        part.take_c(0, 1)
        part.take_c(1, 3)
    part0.event(2)
    t_load.wait()
    s_load.wait()
    part2.crossed(0)
    student_planes(1, lambda i: y)
    part0.event(3)
    for part in both:
        part.take_c(0, 3)
        part.take_c(1, 1)
    part1.crossed(0)
    teacher_x(1, lambda i: x)
    for part in both:
        part.take_c(0, 2)
        part.take_c(1, 2)
    part0.event(4)
    for i in range(4):
        part0.crossed(i)
    teacher_z(1, lambda i: lax.rem(zl + 2, 4))
    part0.event(5)
    part2.crossed(1)
    part2.crossed(3)
    student_planes(2, lambda i: lax.rem(y + 1 + 2 * i, Y))
    for part in both:
        for way, r in ((0, 0), (0, 1), (1, 3), (1, 2)):
            part.take_c(way, r, 1)
    part0.event(6)
    part1.crossed(1)
    part1.crossed(3)
    teacher_x(2, lambda i: lax.rem(x + 1 + 2 * i, X))
    part0.crossed(4)
    part0.crossed(5)
    teacher_z(2, lambda i: lax.rem(zl + 1 + 2 * i, 4))
    part2.crossed(2)
    student_planes(1, lambda i: lax.rem(y + 2, Y))
    part1.crossed(2)
    teacher_x(1, lambda i: lax.rem(x + 2, X))
    part0.crossed(6)
    part0.crossed_own()
    teacher_z(1, lambda i: zl)

    order = []
    for v in range(8):
        order += [t_acc0[v * 16 : v * 16 + 16, :], t_acc1[v * 16 : v * 16 + 16, :]]
    tl = jnp.concatenate(order, axis=0).T
    sl = s_acc[...].T
    t_acc[...] = tl
    s_acc[...] = sl
    column_start = (dp * 8 + vo) * WIDTH
    onehot = (column_start + lax.broadcasted_iota(jnp.int32, (WIDTH, TOKENS), 0) == ids[...]).astype(F32)
    t_top = jnp.max(tl, axis=0, keepdims=True)
    s_top = jnp.max(sl, axis=0, keepdims=True)
    over_v = lambda a: jnp.sum(a, axis=0, keepdims=True)

    def merge(values):
        rows = []
        for k in (0, 2):
            top = functools.reduce(jnp.maximum, [v[k : k + 1] for v in values])
            rows += [top, add_all([v[k + 1 : k + 2] * jnp.exp(v[k : k + 1] - top) for v in values])]
        return pad(rows + [add_all([v[4:5] for v in values])])

    first = []
    finish(
        exchange(
            1,
            pad([t_top, over_v(jnp.exp(tl - t_top)), s_top, over_v(jnp.exp(sl - s_top)), over_v(onehot * sl)]),
            merge,
            first,
        )
    )
    first = first[0]
    t_lse = first[0:1] + jnp.log(first[1:2])
    s_lse = first[2:3] + jnp.log(first[3:4])
    picked = first[4:5]
    t_logp = t_acc[...] - t_lse
    s_logp = s_acc[...] - s_lse
    a, b = math.log(MIX_WEIGHT) + t_logp, math.log(1.0 - MIX_WEIGHT) + s_logp
    mix_logp = jnp.maximum(a, b) + jnp.log1p(jnp.exp(-jnp.abs(a - b)))
    p_, q = jnp.exp(t_logp), jnp.exp(s_logp)
    gap = s_logp - mix_logp
    q_gap = q * gap
    jsd_part = over_v(MIX_WEIGHT * p_ * (t_logp - mix_logp) + (1.0 - MIX_WEIGHT) * q_gap)
    second = []
    finish(
        exchange(
            2,
            pad([jsd_part, over_v(q_gap), over_v(q_gap * s_logp), over_v(q * s_logp)]),
            add_all,
            second,
        )
    )
    second = second[0]
    jsd, kl = second[0:1], second[1:2]
    weights = mask[...].astype(F32)
    count = jnp.sum(weights, axis=1, keepdims=True)
    row_scale = LOSS_SCALE * weights / count
    rest = 1.0 - MIX_WEIGHT
    logit_grad = row_scale * (q * (rest * gap - rest * kl) + NLL_WEIGHT * (q - onehot))
    lg[...] = logit_grad.T.reshape(16, 2, 8, WIDTH)
    lhs = jnp.concatenate([lg[:, 1 - c].reshape(128, WIDTH), lg[:, c].reshape(128, WIDTH)], axis=0).astype(BF16)

    sibling = to_c(1 - c)

    def sib_copy(v):
        return remote(sib_out.at[v], sib_in.at[v], sib_send_sem.at[v], sib_recv_sem.at[v], sibling)

    def grad_step(v, carry):
        y_, zh_ = lax.div(v, 2), lax.rem(v, 2)
        halves = []
        for h in range(2):
            w = s_w[pl.ds(pl.multiple_of(v * 1024 + h * 512, 512), 512), :]
            halves.append(
                lax.dot_general(lhs, w, (((1,), (1,)), ((), ())), preferred_element_type=F32).reshape(2, 16, 8, 512)
            )
        chunks = jnp.concatenate(halves, axis=2)
        sib_out[v] = chunks[0].astype(BF16)
        sib_copy(v).start()
        for i in range(16):
            raf[i % 4, y_, zh_ * 4 + i // 4] = chunks[1, i, :, :256]
            rbf[y_, i % 4, zh_ * 4 + i // 4] = chunks[1, i, :, 256:]
        return carry

    lax.fori_loop(0, 8, grad_step, 0)

    def sib_step(v, carry):
        y_, zh_ = lax.div(v, 2), lax.rem(v, 2)
        sib_copy(v).wait()
        for i in range(16):
            got = sib_in[v, i].astype(F32)
            at_a = (i % 4, y_, zh_ * 4 + i // 4)
            at_b = (y_, i % 4, zh_ * 4 + i // 4)
            sum_a = raf[at_a] + got[:, :256]
            sum_b = rbf[at_b] + got[:, 256:]
            raf[at_a] = sum_a
            rbf[at_b] = sum_b
            ra_out[at_a] = sum_a.astype(BF16)
            rb_out[at_b] = sum_b.astype(BF16)
        return carry

    class First:
        def __init__(self, part, axis, own, out, via, landing):
            self.part, self.own, self.out, self.via, self.landing = part, own, out, via, landing
            _, self.me, to = axis
            self.to = (to(lax.rem(self.me + 1, 4)), to(lax.rem(self.me + 3, 4)))

        def plane(self, k):
            return lax.rem(self.me + k, 4)

        def send(self, way, item):
            half = way if item != 1 else 1 - way
            k = 2 if item == 0 else (1 if way == 0 else 3)
            src = self.out.at[self.plane(k), 2 * half : 2 * half + 2]
            dst = self.via.at[way] if item == 0 else self.landing.at[way, 2 * half : 2 * half + 2]
            start(src, dst, first_send.at[self.part, way, item], first_recv.at[self.part, way, item], self.to[way])

        def take(self, way, item):
            half = way if item != 1 else 1 - way
            dst = self.via.at[way] if item == 0 else self.landing.at[way, 2 * half : 2 * half + 2]
            arrived(dst, first_send.at[self.part, way, item], first_recv.at[self.part, way, item], self.to[way])

        def middle(self):
            for way in range(2):
                self.take(way, 0)
                to = self.plane(1 if way == 0 else 3)

                def step(i, carry, way=way, to=to):
                    row = 2 * way + lax.div(i, 8)
                    at = lax.rem(i, 8)
                    total = self.own[to, row, at] + self.via[way, lax.div(i, 8), at].astype(F32)
                    self.out[to, row, at] = total.astype(BF16)
                    return carry

                lax.fori_loop(0, 16, step, 0, unroll=4)
                self.send(way, 2)

        def last(self, total, out):
            for way in range(2):
                self.take(way, 1)
                self.take(way, 2)

            def step(i, carry):
                row, at = lax.div(i, 8), lax.rem(i, 8)
                value = self.own[self.me, row, at] + (
                    self.landing[0, row, at].astype(F32) + self.landing[1, row, at].astype(F32)
                )
                total[row, at] = value
                out[row, at] = value.astype(BF16)
                return carry

            lax.fori_loop(0, 32, step, 0, unroll=4)

    first_a = First(0, axis_x, raf, ra_out, ra_via, ra_in)
    first_b = First(1, axis_y, rbf, rb_out, rb_via, rb_in)
    lax.fori_loop(0, 4, sib_step, 0)
    first_a.send(0, 0)
    first_a.send(1, 1)
    lax.fori_loop(4, 8, sib_step, 0)
    first_a.send(1, 0)
    for way in range(2):
        first_b.send(way, 0)
    first_a.send(0, 1)
    for way in range(2):
        first_b.send(way, 1)

    def gain_step(v, carry):
        y_, zh_ = lax.div(v, 2), lax.rem(v, 2)
        total = jnp.zeros((16, 512), F32)
        for i in range(16):
            z_ = zh_ * 4 + i // 4
            inv = s_inv[i, c]
            scaled = g2[c, y_, i % 4, z_].astype(F32) * wide(jnp.concatenate([inv, inv], axis=0))
            total += scaled * jnp.concatenate([raf[i % 4, y_, z_], rbf[y_, i % 4, z_]], axis=1)
        pieces = []
        for h in range(2):
            row = jnp.sum(total[8 * h : 8 * h + 8], axis=0, keepdims=True)
            pieces += [row[:, k * 128 : (k + 1) * 128] for k in range(4)]
        gp_c[c, y_, zh_] = jnp.concatenate(pieces, axis=0)
        return carry

    lax.fori_loop(0, 8, gain_step, 0)
    gain_wait = all_partners(
        axis_c, lambda j: gp_c.at[c], lambda j: gp_c.at[j], lambda k: gp_send.at[0, k], lambda j: gp_recv.at[0, j]
    )
    first_a.middle()
    gain_wait()
    gp1[...] = gp_c[0] + gp_c[1]
    gp_y[y] = gp1[y]
    gain_wait = all_partners(
        axis_y, lambda j: gp1.at[j], lambda j: gp_y.at[j], lambda k: gp_send.at[1, k], lambda j: gp_recv.at[1, j]
    )
    first_b.middle()

    def scatter(axis, src, landing, part, phase):
        return all_partners(
            axis,
            lambda j: src.at[j],
            lambda j: landing.at[j],
            lambda k: rs_send.at[part, phase, k],
            lambda j: rs_recv.at[part, phase, j],
        )

    def second_sum(axis, own, landing, total, out):
        n, me, _ = axis
        for at in range(Z):
            value = own[me, at]
            for k in range(1, n):
                value = value + landing[lax.rem(me + k, n), at].astype(F32)
            total[at] = value
            out[at] = value.astype(BF16)

    def third_sum(own, landing):
        value = own[z]
        for k in range(1, Z):
            value = value + landing[lax.rem(z + k, Z)].astype(F32)
        return value

    first_a.last(raf2, ra2)
    wait_a = scatter(axis_y, ra2, ra_in2, 0, 0)
    first_b.last(rbf2, rb2)
    wait_b = scatter(axis_x, rb2, rb_in2, 1, 0)
    gain_wait()
    gp_x[x] = add_all([gp_y[j] for j in range(Y)])
    gain_wait = all_partners(
        axis_x, lambda j: gp_x.at[x], lambda j: gp_x.at[j], lambda k: gp_send.at[2, k], lambda j: gp_recv.at[2, j]
    )

    row_dot = row_scale * (
        rest * (second[2:3] - kl * second[3:4]) + NLL_WEIGHT * (second[3:4] - (picked - s_lse))
    ) / DS
    dot_col[...] = column(row_dot).reshape(dot_col.shape)
    loss = jnp.sum(weights * (jsd + NLL_WEIGHT * (s_lse - picked)), axis=1, keepdims=True) / count
    loss_out[...] = jnp.broadcast_to(loss, loss_out.shape)

    wait_a()
    second_sum(axis_y, raf2, ra_in2, raf3, ra3)
    wait_a = scatter(axis_z, ra3, ra_in3, 0, 1)
    wait_b()
    second_sum(axis_x, rbf2, rb_in2, rbf3, rb3)
    wait_b = scatter(axis_z, rb3, rb_in3, 1, 1)
    gain_wait()
    gp3[...] = add_all([gp_x[j] for j in range(X)])
    gp_z[z] = gp3[zh]
    gain_wait = all_partners(
        axis_z,
        lambda j: gp3.at[lax.div(j, 4)],
        lambda j: gp_z.at[j],
        lambda k: gp_send.at[3, k],
        lambda j: gp_recv.at[3, j],
    )
    wait_a()
    wait_b()
    normed_grad = jnp.concatenate([third_sum(raf3, ra_in3), third_sum(rbf3, rb_in3)], axis=1)
    inv = wide(s_inv[lax.div(dp, 2), c])
    dots = wide(dot_col[lax.div(dp, 2), c])
    for h in range(2):
        grad = normed_grad[h * 8 : h * 8 + 8]
        scaled = own_rows[:, h * 512 : (h + 1) * 512] * inv
        gain = s_gain[pl.ds(vo * 2 + h, 1), :]
        grad_out[:, h * 512 : (h + 1) * 512] = inv * (grad * gain - scaled * dots)
    gain_wait()
    gain_out[...] = add_all([gp_z[j] for j in range(Z)])
    for copy in late:
        copy.wait_send()


def results(loss, grad, gain, loss_out, grad_out, gain_out):
    loss_out[...] = loss[...]
    grad_out[...] = grad[...].astype(BF16)
    gain_out[...] = gain[...]


def shards(t_rows, t_gain, t_head, s_rows, s_gain, s_head, ids, mask):
    vmem = pl.BlockSpec(memory_space=pltpu.VMEM)
    hbm = pl.BlockSpec(memory_space=pl.ANY)
    dma = pltpu.SemaphoreType.DMA
    scratch = [
        pltpu.VMEM((2, Z, X * Y, 16, 512), BF16),
        pltpu.VMEM((2, X, Y, Z, 16, 512), BF16),
        pltpu.VMEM((2, Y, X, Z, 16, 512), BF16),
        pltpu.VMEM((DT, WIDTH), BF16),
        pltpu.VMEM((DS, WIDTH), BF16),
        pltpu.VMEM((DT // 512, 512), F32),
        pltpu.VMEM((DS // 512, 512), F32),
        pltpu.VMEM((TOKENS, 128), F32),
        pltpu.VMEM((16, 2, 8, 128), F32),
        pltpu.VMEM((TOKENS // 2, WIDTH), F32),
        pltpu.VMEM((TOKENS // 2, WIDTH), F32),
        pltpu.VMEM((TOKENS, WIDTH), F32),
        pltpu.VMEM((TOKENS, WIDTH), F32),
        pltpu.VMEM((16, 2, 8, 128), F32),
        pltpu.VMEM((16, 2, 8, WIDTH), F32),
        pltpu.VMEM((8, 16, 16, 512), BF16),
        pltpu.VMEM((8, 16, 16, 512), BF16),
        pltpu.VMEM((X, Y, Z, 16, 256), F32),
        pltpu.VMEM((Y, X, Z, 16, 256), F32),
        pltpu.VMEM((X, Y, Z, 16, 256), BF16),
        pltpu.VMEM((Y, X, Z, 16, 256), BF16),
        pltpu.VMEM((2, 2, Z, 16, 256), BF16),
        pltpu.VMEM((2, 2, Z, 16, 256), BF16),
        pltpu.VMEM((2, Y, Z, 16, 256), BF16),
        pltpu.VMEM((2, X, Z, 16, 256), BF16),
        pltpu.VMEM((Y, Z, 16, 256), F32),
        pltpu.VMEM((X, Z, 16, 256), F32),
        pltpu.VMEM((Y, Z, 16, 256), BF16),
        pltpu.VMEM((X, Z, 16, 256), BF16),
        pltpu.VMEM((Y, Z, 16, 256), BF16),
        pltpu.VMEM((X, Z, 16, 256), BF16),
        pltpu.VMEM((Z, 16, 256), F32),
        pltpu.VMEM((Z, 16, 256), F32),
        pltpu.VMEM((Z, 16, 256), BF16),
        pltpu.VMEM((Z, 16, 256), BF16),
        pltpu.VMEM((Z, 16, 256), BF16),
        pltpu.VMEM((Z, 16, 256), BF16),
        pltpu.VMEM((3, 2, 8, TOKENS), F32),
        pltpu.VMEM((3, X * Y, 8, TOKENS), F32),
        pltpu.VMEM((3, Z, 8, TOKENS), F32),
        pltpu.VMEM((2, Y, 2, 8, 128), F32),
        pltpu.VMEM((Y, 2, 8, 128), F32),
        pltpu.VMEM((Y, 2, 8, 128), F32),
        pltpu.VMEM((X, 2, 8, 128), F32),
        pltpu.VMEM((2, 8, 128), F32),
        pltpu.VMEM((Z, 8, 128), F32),
        dma((2,)),
        dma((3, 16)),
        dma((3, 16)),
        dma((3, 2, 2)),
        dma((3, 2, 2)),
        dma((3, 2, 8)),
        dma((3, 2, 8)),
        dma((3, 16)),
        dma((3, 16)),
        dma((3, 26)),
        dma((3, 26)),
        dma((8,)),
        dma((8,)),
        dma((2, 2, 3)),
        dma((2, 2, 3)),
        dma((2, 2, 8)),
        dma((2, 2, 8)),
        dma((4, 8)),
        dma((4, 8)),
    ]
    flops = 2 * TOKENS * WIDTH * (DT + 2 * DS)
    shapes = (
        jax.ShapeDtypeStruct((8, 128), F32),
        jax.ShapeDtypeStruct(s_rows.shape, F32),
        jax.ShapeDtypeStruct((8, 128), F32),
    )
    values = pl.pallas_call(
        kernel,
        out_shape=shapes,
        in_specs=[vmem, vmem, hbm, vmem, vmem, hbm, vmem, vmem],
        out_specs=(vmem, vmem, vmem),
        scratch_shapes=scratch,
        compiler_params=pltpu.CompilerParams(
            collective_id=0, has_side_effects=True, vmem_limit_bytes=60 * 1024 * 1024
        ),
        cost_estimate=pl.CostEstimate(flops=flops, bytes_accessed=2 * WIDTH * (DT + DS), transcendentals=0),
    )(t_rows, t_gain, t_head, s_rows, s_gain, s_head, ids.reshape(1, TOKENS), mask.reshape(1, TOKENS))
    loss, grad, gain = pl.pallas_call(
        results,
        out_shape=(shapes[0], jax.ShapeDtypeStruct(s_rows.shape, BF16), shapes[2]),
        in_specs=[vmem] * 3,
        out_specs=(vmem, vmem, vmem),
    )(*values)
    return loss[0, 0], grad, gain.reshape(1024)


def solution(mesh):
    return jax.shard_map(
        shards,
        mesh=mesh,
        in_specs=(
            P("vocab", "dp"),
            P(),
            P(None, ("dp", "vocab")),
            P("dp", "vocab"),
            P(),
            P(None, ("dp", "vocab")),
            P(),
            P(),
        ),
        out_specs=(P(), P("dp", "vocab"), P("vocab")),
        check_vma=False,
    )
```

time: 141 us -> 112 us (0.79); the launches traced: 139 us -> 111 us
  Pallas kernels: 131 us -> 110 us
  local copies, waits for them, and re-layouts: 5.21 us -> 1.19 us
    pallas_call x1 -> x2, Pallas kernels: 131 us -> 110 us  [the longest x1 108 us: shards(): pl.pallas_call(kernel, out_shape=shapes, in_specs=[vmem, vmem, hbm, vmem,...]
    reshape x2 -> x0, local copies, waits for them, and re-layouts: 2.75 us -> none  [the longest x1 1.4 us: shards(): t_gain.astype(F32).reshape(DT // 512, 512)]
where the time goes in v2:
time: 112 us; the launch traced here: 111 us
  Pallas kernels  110 us (98%)
  local copies, waits for them, and re-layouts  1.19 us (1%)
    pallas_call x1, Pallas kernels, shards(): pl.pallas_call(kernel, out_shape=shapes, in_specs=[vmem, vmem, hbm, vmem,...  108 us

profile of v2, /device:TPU:32, one launch (start us, length us, event | category | flops | bytes accessed | tf_op | source)
XLA Modules:
  0.0 111.5 jit_solution(10461796106054000671)
XLA Ops:
  0.6 108.3 %shard_map.103 = (f32[8,128]{1,0:T(8,128)}, f32[8,1024]{1,0:T(8,128)}, f32[8,128]{1,0:T(8,128)}) custom-call(bf16[32,512]{1,0:T(8,128)(2,1)} %t_rows.1, bf16[16384]{0:T(1024)(128)(2,1)} %t_gain_in.1, bf16[16384,256]{1,0:T(8,128)(2,1)} %t_head.1, bf16[8,1024]{1,0:T(8,128)(2,1)} %s_rows.1, bf16[8192]{0:T(1024)(128)(2,1)} %s_gain_in.1, ...), custom_call_target="tpu_custom_call" | custom-call | flops 4294967296 | bytes 12582912 | tf_op jit(solution)/shard_map/pallas_call | solution.py:738
  108.9 1.4 %shard_map.104 = (f32[8,128]{1,0:T(8,128)}, bf16[8,1024]{1,0:T(8,128)(2,1)}, f32[8,128]{1,0:T(8,128)}) custom-call(f32[8,128]{1,0:T(8,128)} %get-tuple-element.9.loss, f32[8,1024]{1,0:T(8,128)} %get-tuple-element.10.grad, f32[8,128]{1,0:T(8,128)} %get-tuple-element.11.gain), custom_call_target="tpu_custom_call" | custom-call | tf_op jit(solution)/shard_map/pallas_call | solution.py:749
  110.3 1.2 %slice.3 = f32[1,1]{1,0:T(1,128)} slice(f32[8,128]{1,0:T(8,128)} %get-tuple-element.12), slice={[0:1], [0:1]} | slice | bytes 8 | tf_op jit(solution)/shard_map/slice | solution.py:755

commit v3 on v2

--- a/solution.py
+++ b/solution.py
@@ -56,6 +56,11 @@
             pl.semaphore_signal(barrier, inc=1, device_id=to(lax.rem(me + k, n)), device_id_type=MESH)
             partners += 1
 
+    t_load = pltpu.make_async_copy(t_head, t_w, head_sem.at[0])
+    s_load = pltpu.make_async_copy(s_head, s_w, head_sem.at[1])
+    t_load.start()
+    s_load.start()
+
     def remote(src, dst, send, recv, to):
         return pltpu.make_async_remote_copy(
             src_ref=src, dst_ref=dst, send_sem=send, recv_sem=recv, device_id=to, device_id_type=MESH
@@ -88,8 +93,20 @@
     t_own = t_rows[...].astype(F32)
     t_squares = jnp.where(lax.div(lanes, 32) == vo, lane_sums(t_own * t_own), 0.0)
     s_squares = jnp.where(lax.div(lanes, 8) == dp, lane_sums(own_rows * own_rows), 0.0)
-    pad = lambda rows: jnp.concatenate(rows + [jnp.zeros((8 - len(rows), TOKENS), F32)], axis=0)
-    squares_value = pad([t_squares, s_squares])
+
+    def pack(rows):
+        halves = [row[:, 128 * h : 128 * h + 128] for row in rows for h in range(2)]
+        return jnp.concatenate(halves + [jnp.zeros((1, 128), F32)] * (8 - len(halves)), axis=0)
+
+    def unpack(block, k):
+        return jnp.concatenate([block[2 * k : 2 * k + 1], block[2 * k + 1 : 2 * k + 2]], axis=1)
+
+    squares_value = pack([t_squares, s_squares])
+
+    t_gain[...] = t_gain_in[...].astype(F32).reshape(t_gain.shape)
+    s_gain[...] = s_gain_in[...].astype(F32).reshape(s_gain.shape)
+    for acc in (t_acc0, t_acc1, s_acc):
+        acc[...] = jnp.zeros_like(acc)
 
     pl.semaphore_wait(barrier, partners)
 
@@ -107,9 +124,10 @@
 
         return wait
 
-    def exchange(r, value, combine, result):
-        base = 0
-        for axis, buf in ((axis_c, st_c), (axis_p, st_p), (axis_z, st_z)):
+    over_c, over_p, over_z = (axis_c, st_c, 0), (axis_p, st_p, 2), (axis_z, st_z, 18)
+
+    def exchange(r, value, combine, result, steps=(over_c, over_p, over_z)):
+        for axis, buf, base in steps:
             n, me, _ = axis
             buf[r, me] = value
             wait = all_partners(
@@ -122,7 +140,6 @@
             yield
             wait()
             value = combine([buf[r, j] for j in range(n)])
-            base += n
         result.append(value)
 
     def finish(steps):
@@ -274,33 +291,39 @@
 
         lax.fori_loop(0, 2 * count, step, 0)
 
-    def teacher_step(acc, p, load, d):
-        gain = t_gain[pl.ds(d, 1), :]
-        blocks = []
+    def teacher_step(acc, p, load, first, count):
+        lhs = []
         for v in range(8):
             inv = wide(t_inv[v * 32 + p * 16 : v * 32 + p * 16 + 16, :])
-            blocks.append((load(v).astype(F32) * inv * gain).astype(BF16))
-        w = t_w[pl.ds(pl.multiple_of(d * 512, 512), 512), :]
-        acc[...] += jnp.dot(jnp.concatenate(blocks, axis=0), w, preferred_element_type=F32)
+            blocks = []
+            for k in range(count):
+                gain = t_gain[pl.ds(first + k, 1), :]
+                blocks.append((load(v, k).astype(F32) * inv * gain).astype(BF16))
+            lhs.append(jnp.concatenate(blocks, axis=1))
+        w = t_w[pl.ds(pl.multiple_of(first * 512, 512), count * 512), :]
+        acc[...] += jnp.dot(jnp.concatenate(lhs, axis=0), w, preferred_element_type=F32)
 
     def teacher_x(count, plane_of):
         def step(i, carry):
-            x_, zl_, c_ = plane_of(lax.div(i, 8)), lax.div(lax.rem(i, 8), 2), lax.rem(i, 2)
-            load = lambda v: g1[c_, x_, v // 2, (v % 2) * 4 + zl_]
-            teacher_step(t_acc1, 1, load, (zl_ * X + x_) * 2 + c_)
+            x_, zl_ = plane_of(lax.div(i, 4)), lax.rem(i, 4)
+            load = lambda v, k: g1[k, x_, v // 2, (v % 2) * 4 + zl_]
+            teacher_step(t_acc1, 1, load, (zl_ * X + x_) * 2, 2)
             return carry
 
-        lax.fori_loop(0, 8 * count, step, 0)
+        lax.fori_loop(0, 4 * count, step, 0, unroll=2)
 
     def teacher_z(count, plane_of):
         def step(i, carry):
-            zl_, x_, c_ = plane_of(lax.div(i, 8)), lax.div(lax.rem(i, 8), 2), lax.rem(i, 2)
-            load = lambda v: g0[c_, (v % 2) * 4 + zl_, x_ * Y + v // 2]
-            teacher_step(t_acc0, 0, load, (zl_ * X + x_) * 2 + c_)
+            zl_, x_ = plane_of(lax.div(i, 2)), 2 * lax.rem(i, 2)
+            load = lambda v, k: g0[k % 2, (v % 2) * 4 + zl_, (x_ + k // 2) * Y + v // 2]
+            teacher_step(t_acc0, 0, load, (zl_ * X + x_) * 2, 4)
             return carry
 
-        lax.fori_loop(0, 8 * count, step, 0)
-
+        lax.fori_loop(0, 2 * count, step, 0)
+
+    squares = []
+    round0 = exchange(0, squares_value, add_all, squares, (over_z, over_c, over_p))
+    next(round0)
     for part in both:
         part.begin()
     wait_plane = all_partners(
@@ -310,22 +333,13 @@
         lambda k: a_send.at[0, k],
         lambda j: a_recv.at[0, j],
     )
-    t_load = pltpu.make_async_copy(t_head, t_w, head_sem.at[0])
-    s_load = pltpu.make_async_copy(s_head, s_w, head_sem.at[1])
-    t_load.start()
-    s_load.start()
-    squares = []
-    round0 = exchange(0, squares_value, add_all, squares)
     next(round0)
-    t_gain[...] = t_gain_in[...].astype(F32).reshape(t_gain.shape)
-    s_gain[...] = s_gain_in[...].astype(F32).reshape(s_gain.shape)
-    for acc in (t_acc0, t_acc1, s_acc):
-        acc[...] = jnp.zeros_like(acc)
     next(round0)
-    for part in both:
-        part.after_a()
     wait_plane()
     part0.begin()
+    for part in both:
+        part.after_a()
+    part0.event(0)
     for part in both:
         part.take_b(0)
     for part in both:
@@ -333,60 +347,62 @@
         part.take_c(1, 0)
         part.send_c(0, 3)
         part.send_c(1, 1)
-    next(round0)
-    part0.event(0)
     part0.event(1)
-    for part in both:
-        part.take_b(1)
     finish(round0)
     squares = squares[0]
-    t_inv_row = lax.rsqrt(squares[0:1] / DT + EPSILON)
-    s_inv_row = lax.rsqrt(squares[1:2] / DS + EPSILON)
+    t_inv_row = lax.rsqrt(unpack(squares, 0) / DT + EPSILON)
+    s_inv_row = lax.rsqrt(unpack(squares, 1) / DS + EPSILON)
     column = lambda row: jnp.broadcast_to(row, (128, TOKENS)).T
     t_inv[...] = column(t_inv_row)
     s_inv[...] = column(s_inv_row).reshape(s_inv.shape)
+    t_load.wait()
+    s_load.wait()
+    for part in both:
+        part.take_b(1)
+    part0.event(2)
     for part in both:
         part.take_c(0, 1)
         part.take_c(1, 3)
-    part0.event(2)
-    t_load.wait()
-    s_load.wait()
+    part0.event(3)
     part2.crossed(0)
     student_planes(1, lambda i: y)
-    part0.event(3)
     for part in both:
         part.take_c(0, 3)
         part.take_c(1, 1)
+    part0.event(4)
     part1.crossed(0)
     teacher_x(1, lambda i: x)
     for part in both:
         part.take_c(0, 2)
         part.take_c(1, 2)
-    part0.event(4)
     for i in range(4):
         part0.crossed(i)
     teacher_z(1, lambda i: lax.rem(zl + 2, 4))
     part0.event(5)
+    for part in both:
+        for way, r in ((0, 0), (1, 3)):
+            part.take_c(way, r, 1)
     part2.crossed(1)
     part2.crossed(3)
     student_planes(2, lambda i: lax.rem(y + 1 + 2 * i, Y))
     for part in both:
-        for way, r in ((0, 0), (0, 1), (1, 3), (1, 2)):
-            part.take_c(way, r, 1)
+        part.take_c(0, 1, 1)
+    part0.crossed(4)
+    part0.crossed(5)
+    teacher_z(2, lambda i: lax.rem(zl + 1 + 2 * i, 4))
     part0.event(6)
     part1.crossed(1)
     part1.crossed(3)
     teacher_x(2, lambda i: lax.rem(x + 1 + 2 * i, X))
-    part0.crossed(4)
-    part0.crossed(5)
-    teacher_z(2, lambda i: lax.rem(zl + 1 + 2 * i, 4))
+    for part in both:
+        part.take_c(1, 2, 1)
+    part0.crossed(6)
+    part0.crossed_own()
+    teacher_z(1, lambda i: zl)
     part2.crossed(2)
     student_planes(1, lambda i: lax.rem(y + 2, Y))
     part1.crossed(2)
     teacher_x(1, lambda i: lax.rem(x + 2, X))
-    part0.crossed(6)
-    part0.crossed_own()
-    teacher_z(1, lambda i: zl)
 
     order = []
     for v in range(8):
@@ -402,25 +418,15 @@
     over_v = lambda a: jnp.sum(a, axis=0, keepdims=True)
 
     def merge(values):
-        rows = []
-        for k in (0, 2):
-            top = functools.reduce(jnp.maximum, [v[k : k + 1] for v in values])
-            rows += [top, add_all([v[k + 1 : k + 2] * jnp.exp(v[k : k + 1] - top) for v in values])]
-        return pad(rows + [add_all([v[4:5] for v in values])])
+        top = functools.reduce(jnp.maximum, [v[0:4] for v in values])
+        return jnp.concatenate([top, add_all([v[4:8] * jnp.exp(v[0:4] - top) for v in values])], axis=0)
 
     first = []
-    finish(
-        exchange(
-            1,
-            pad([t_top, over_v(jnp.exp(tl - t_top)), s_top, over_v(jnp.exp(sl - s_top)), over_v(onehot * sl)]),
-            merge,
-            first,
-        )
-    )
+    value = pack([t_top, s_top, over_v(jnp.exp(tl - t_top)), over_v(jnp.exp(sl - s_top))])
+    finish(exchange(1, value, merge, first))
     first = first[0]
-    t_lse = first[0:1] + jnp.log(first[1:2])
-    s_lse = first[2:3] + jnp.log(first[3:4])
-    picked = first[4:5]
+    t_lse = unpack(first, 0) + jnp.log(unpack(first, 2))
+    s_lse = unpack(first, 1) + jnp.log(unpack(first, 3))
     t_logp = t_acc[...] - t_lse
     s_logp = s_acc[...] - s_lse
     a, b = math.log(MIX_WEIGHT) + t_logp, math.log(1.0 - MIX_WEIGHT) + s_logp
@@ -428,22 +434,18 @@
     p_, q = jnp.exp(t_logp), jnp.exp(s_logp)
     gap = s_logp - mix_logp
     q_gap = q * gap
-    jsd_part = over_v(MIX_WEIGHT * p_ * (t_logp - mix_logp) + (1.0 - MIX_WEIGHT) * q_gap)
+    weights = mask[...].astype(F32)
+    rest = 1.0 - MIX_WEIGHT
+    loss_part = weights * over_v(
+        MIX_WEIGHT * p_ * (t_logp - mix_logp) + rest * q_gap - NLL_WEIGHT * (onehot * s_logp)
+    )
+    dot_part = over_v((rest * q_gap + NLL_WEIGHT * (q - onehot)) * s_logp)
     second = []
-    finish(
-        exchange(
-            2,
-            pad([jsd_part, over_v(q_gap), over_v(q_gap * s_logp), over_v(q * s_logp)]),
-            add_all,
-            second,
-        )
-    )
+    finish(exchange(2, pack([loss_part, over_v(q_gap), dot_part, over_v(q * s_logp)]), add_all, second))
     second = second[0]
-    jsd, kl = second[0:1], second[1:2]
-    weights = mask[...].astype(F32)
+    kl = unpack(second, 1)
     count = jnp.sum(weights, axis=1, keepdims=True)
     row_scale = LOSS_SCALE * weights / count
-    rest = 1.0 - MIX_WEIGHT
     logit_grad = row_scale * (q * (rest * gap - rest * kl) + NLL_WEIGHT * (q - onehot))
     lg[...] = logit_grad.T.reshape(16, 2, 8, WIDTH)
     lhs = jnp.concatenate([lg[:, 1 - c].reshape(128, WIDTH), lg[:, c].reshape(128, WIDTH)], axis=0).astype(BF16)
@@ -453,8 +455,12 @@
     def sib_copy(v):
         return remote(sib_out.at[v], sib_in.at[v], sib_send_sem.at[v], sib_recv_sem.at[v], sibling)
 
-    def grad_step(v, carry):
-        y_, zh_ = lax.div(v, 2), lax.rem(v, 2)
+    def place(i):
+        return lax.rem(y + 2 + 3 * i, Y), lax.div(i, 4)
+
+    def grad_step(i, carry):
+        y_, zh_ = place(i)
+        v = y_ * 2 + zh_
         halves = []
         for h in range(2):
             w = s_w[pl.ds(pl.multiple_of(v * 1024 + h * 512, 512), 512), :]
@@ -464,20 +470,19 @@
         chunks = jnp.concatenate(halves, axis=2)
         sib_out[v] = chunks[0].astype(BF16)
         sib_copy(v).start()
-        for i in range(16):
-            raf[i % 4, y_, zh_ * 4 + i // 4] = chunks[1, i, :, :256]
-            rbf[y_, i % 4, zh_ * 4 + i // 4] = chunks[1, i, :, 256:]
+        for k in range(16):
+            raf[k % 4, zh_, y_, k // 4] = chunks[1, k, :, :256]
+            rbf[y_, zh_, k % 4, k // 4] = chunks[1, k, :, 256:]
         return carry
 
-    lax.fori_loop(0, 8, grad_step, 0)
-
-    def sib_step(v, carry):
-        y_, zh_ = lax.div(v, 2), lax.rem(v, 2)
+    def sib_step(i, carry):
+        y_, zh_ = place(i)
+        v = y_ * 2 + zh_
         sib_copy(v).wait()
-        for i in range(16):
-            got = sib_in[v, i].astype(F32)
-            at_a = (i % 4, y_, zh_ * 4 + i // 4)
-            at_b = (y_, i % 4, zh_ * 4 + i // 4)
+        for k in range(16):
+            got = sib_in[v, k].astype(F32)
+            at_a = (k % 4, zh_, y_, k // 4)
+            at_b = (y_, zh_, k % 4, k // 4)
             sum_a = raf[at_a] + got[:, :256]
             sum_b = rbf[at_b] + got[:, 256:]
             raf[at_a] = sum_a
@@ -498,29 +503,27 @@
         def send(self, way, item):
             half = way if item != 1 else 1 - way
             k = 2 if item == 0 else (1 if way == 0 else 3)
-            src = self.out.at[self.plane(k), 2 * half : 2 * half + 2]
-            dst = self.via.at[way] if item == 0 else self.landing.at[way, 2 * half : 2 * half + 2]
+            src = self.out.at[self.plane(k), half]
+            dst = self.via.at[way] if item == 0 else self.landing.at[way, half]
             start(src, dst, first_send.at[self.part, way, item], first_recv.at[self.part, way, item], self.to[way])
 
         def take(self, way, item):
             half = way if item != 1 else 1 - way
-            dst = self.via.at[way] if item == 0 else self.landing.at[way, 2 * half : 2 * half + 2]
+            dst = self.via.at[way] if item == 0 else self.landing.at[way, half]
             arrived(dst, first_send.at[self.part, way, item], first_recv.at[self.part, way, item], self.to[way])
 
-        def middle(self):
-            for way in range(2):
-                self.take(way, 0)
-                to = self.plane(1 if way == 0 else 3)
-
-                def step(i, carry, way=way, to=to):
-                    row = 2 * way + lax.div(i, 8)
-                    at = lax.rem(i, 8)
-                    total = self.own[to, row, at] + self.via[way, lax.div(i, 8), at].astype(F32)
-                    self.out[to, row, at] = total.astype(BF16)
-                    return carry
-
-                lax.fori_loop(0, 16, step, 0, unroll=4)
-                self.send(way, 2)
+        def middle(self, way):
+            self.take(way, 0)
+            to = self.plane(1 if way == 0 else 3)
+
+            def step(i, carry):
+                row, at = lax.div(i, 4), lax.rem(i, 4)
+                total = self.own[to, way, row, at] + self.via[way, row, at].astype(F32)
+                self.out[to, way, row, at] = total.astype(BF16)
+                return carry
+
+            lax.fori_loop(0, 16, step, 0, unroll=4)
+            self.send(way, 2)
 
         def last(self, total, out):
             for way in range(2):
@@ -528,28 +531,34 @@
                 self.take(way, 2)
 
             def step(i, carry):
-                row, at = lax.div(i, 8), lax.rem(i, 8)
-                value = self.own[self.me, row, at] + (
-                    self.landing[0, row, at].astype(F32) + self.landing[1, row, at].astype(F32)
-                )
-                total[row, at] = value
-                out[row, at] = value.astype(BF16)
+                row, zl_ = lax.div(i, 4), lax.rem(i, 4)
+                for zh_ in range(2):
+                    value = self.own[self.me, zh_, row, zl_] + (
+                        self.landing[0, zh_, row, zl_].astype(F32) + self.landing[1, zh_, row, zl_].astype(F32)
+                    )
+                    total[row, zh_ * 4 + zl_] = value
+                    out[row, zh_ * 4 + zl_] = value.astype(BF16)
                 return carry
 
-            lax.fori_loop(0, 32, step, 0, unroll=4)
+            lax.fori_loop(0, 16, step, 0, unroll=2)
 
     first_a = First(0, axis_x, raf, ra_out, ra_via, ra_in)
     first_b = First(1, axis_y, rbf, rb_out, rb_via, rb_in)
-    lax.fori_loop(0, 4, sib_step, 0)
+    lax.fori_loop(0, 4, grad_step, 0)
+    lax.fori_loop(0, 1, sib_step, 0)
+    first_b.send(0, 0)
+    lax.fori_loop(4, 8, grad_step, 0)
+    lax.fori_loop(1, 4, sib_step, 0)
     first_a.send(0, 0)
     first_a.send(1, 1)
-    lax.fori_loop(4, 8, sib_step, 0)
+    first_b.send(1, 1)
+    lax.fori_loop(4, 5, sib_step, 0)
+    first_b.send(1, 0)
+    lax.fori_loop(5, 6, sib_step, 0)
+    first_b.send(0, 1)
+    lax.fori_loop(6, 8, sib_step, 0)
     first_a.send(1, 0)
-    for way in range(2):
-        first_b.send(way, 0)
     first_a.send(0, 1)
-    for way in range(2):
-        first_b.send(way, 1)
 
     def gain_step(v, carry):
         y_, zh_ = lax.div(v, 2), lax.rem(v, 2)
@@ -558,7 +567,7 @@
             z_ = zh_ * 4 + i // 4
             inv = s_inv[i, c]
             scaled = g2[c, y_, i % 4, z_].astype(F32) * wide(jnp.concatenate([inv, inv], axis=0))
-            total += scaled * jnp.concatenate([raf[i % 4, y_, z_], rbf[y_, i % 4, z_]], axis=1)
+            total += scaled * jnp.concatenate([raf[i % 4, zh_, y_, i // 4], rbf[y_, zh_, i % 4, i // 4]], axis=1)
         pieces = []
         for h in range(2):
             row = jnp.sum(total[8 * h : 8 * h + 8], axis=0, keepdims=True)
@@ -566,18 +575,21 @@
         gp_c[c, y_, zh_] = jnp.concatenate(pieces, axis=0)
         return carry
 
-    lax.fori_loop(0, 8, gain_step, 0)
+    lax.fori_loop(0, 4, gain_step, 0)
+    first_b.middle(0)
+    first_a.middle(0)
+    lax.fori_loop(4, 8, gain_step, 0)
     gain_wait = all_partners(
         axis_c, lambda j: gp_c.at[c], lambda j: gp_c.at[j], lambda k: gp_send.at[0, k], lambda j: gp_recv.at[0, j]
     )
-    first_a.middle()
+    first_b.middle(1)
+    first_a.middle(1)
     gain_wait()
     gp1[...] = gp_c[0] + gp_c[1]
     gp_y[y] = gp1[y]
     gain_wait = all_partners(
         axis_y, lambda j: gp1.at[j], lambda j: gp_y.at[j], lambda k: gp_send.at[1, k], lambda j: gp_recv.at[1, j]
     )
-    first_b.middle()
 
     def scatter(axis, src, landing, part, phase):
         return all_partners(
@@ -613,11 +625,9 @@
         axis_x, lambda j: gp_x.at[x], lambda j: gp_x.at[j], lambda k: gp_send.at[2, k], lambda j: gp_recv.at[2, j]
     )
 
-    row_dot = row_scale * (
-        rest * (second[2:3] - kl * second[3:4]) + NLL_WEIGHT * (second[3:4] - (picked - s_lse))
-    ) / DS
+    row_dot = row_scale * (unpack(second, 2) - rest * kl * unpack(second, 3)) / DS
     dot_col[...] = column(row_dot).reshape(dot_col.shape)
-    loss = jnp.sum(weights * (jsd + NLL_WEIGHT * (s_lse - picked)), axis=1, keepdims=True) / count
+    loss = jnp.sum(unpack(second, 0), axis=1, keepdims=True) / count
     loss_out[...] = jnp.broadcast_to(loss, loss_out.shape)
 
     wait_a()
@@ -653,7 +663,7 @@
 
 
 def results(loss, grad, gain, loss_out, grad_out, gain_out):
-    loss_out[...] = loss[...]
+    loss_out[0, 0] = loss[0, 0]
     grad_out[...] = grad[...].astype(BF16)
     gain_out[...] = gain[...]
 
@@ -680,14 +690,14 @@
         pltpu.VMEM((16, 2, 8, WIDTH), F32),
         pltpu.VMEM((8, 16, 16, 512), BF16),
         pltpu.VMEM((8, 16, 16, 512), BF16),
-        pltpu.VMEM((X, Y, Z, 16, 256), F32),
-        pltpu.VMEM((Y, X, Z, 16, 256), F32),
-        pltpu.VMEM((X, Y, Z, 16, 256), BF16),
-        pltpu.VMEM((Y, X, Z, 16, 256), BF16),
-        pltpu.VMEM((2, 2, Z, 16, 256), BF16),
-        pltpu.VMEM((2, 2, Z, 16, 256), BF16),
-        pltpu.VMEM((2, Y, Z, 16, 256), BF16),
-        pltpu.VMEM((2, X, Z, 16, 256), BF16),
+        pltpu.VMEM((X, 2, Y, 4, 16, 256), F32),
+        pltpu.VMEM((Y, 2, X, 4, 16, 256), F32),
+        pltpu.VMEM((X, 2, Y, 4, 16, 256), BF16),
+        pltpu.VMEM((Y, 2, X, 4, 16, 256), BF16),
+        pltpu.VMEM((2, 4, 4, 16, 256), BF16),
+        pltpu.VMEM((2, 4, 4, 16, 256), BF16),
+        pltpu.VMEM((2, 2, Y, 4, 16, 256), BF16),
+        pltpu.VMEM((2, 2, X, 4, 16, 256), BF16),
         pltpu.VMEM((Y, Z, 16, 256), F32),
         pltpu.VMEM((X, Z, 16, 256), F32),
         pltpu.VMEM((Y, Z, 16, 256), BF16),
@@ -700,9 +710,9 @@
         pltpu.VMEM((Z, 16, 256), BF16),
         pltpu.VMEM((Z, 16, 256), BF16),
         pltpu.VMEM((Z, 16, 256), BF16),
-        pltpu.VMEM((3, 2, 8, TOKENS), F32),
-        pltpu.VMEM((3, X * Y, 8, TOKENS), F32),
-        pltpu.VMEM((3, Z, 8, TOKENS), F32),
+        pltpu.VMEM((3, 2, 8, 128), F32),
+        pltpu.VMEM((3, X * Y, 8, 128), F32),
+        pltpu.VMEM((3, Z, 8, 128), F32),
         pltpu.VMEM((2, Y, 2, 8, 128), F32),
         pltpu.VMEM((Y, 2, 8, 128), F32),
         pltpu.VMEM((Y, 2, 8, 128), F32),
@@ -748,11 +758,11 @@
     )(t_rows, t_gain, t_head, s_rows, s_gain, s_head, ids.reshape(1, TOKENS), mask.reshape(1, TOKENS))
     loss, grad, gain = pl.pallas_call(
         results,
-        out_shape=(shapes[0], jax.ShapeDtypeStruct(s_rows.shape, BF16), shapes[2]),
+        out_shape=(jax.ShapeDtypeStruct((1, 1), F32), jax.ShapeDtypeStruct(s_rows.shape, BF16), shapes[2]),
         in_specs=[vmem] * 3,
-        out_specs=(vmem, vmem, vmem),
+        out_specs=(pl.BlockSpec(memory_space=pltpu.SMEM), vmem, vmem),
     )(*values)
-    return loss[0, 0], grad, gain.reshape(1024)
+    return loss.reshape(()), grad, gain.reshape(1024)
 
 
 def solution(mesh):

time: 112 us -> 103 us (0.920)
  Pallas kernels: 110 us -> 102 us
  local copies, waits for them, and re-layouts: 1.19 us -> 0 us
    pallas_call x1, Pallas kernels: 108 us -> 100 us  [shards(): pl.pallas_call(kernel, out_shape=shapes, in_specs=[vmem, vmem, hbm, vmem,...]
    slice x1 -> x0, local copies, waits for them, and re-layouts: 1.19 us -> none  [shards(): return (loss[0, 0], grad, gain.reshape(1024))]
where the time goes in v3:
time: 103 us; the launch traced here: 102 us
  Pallas kernels  102 us (99%)
    pallas_call x1, Pallas kernels, shards(): pl.pallas_call(kernel, out_shape=shapes, in_specs=[vmem, vmem, hbm, vmem,...  100 us

profile of v3, /device:TPU:32, one launch (start us, length us, event | category | flops | bytes accessed | tf_op | source)
XLA Modules:
  0.0 102.3 jit_solution(748481856507839251)
XLA Ops:
  0.6 100.2 %shard_map.103 = (f32[8,128]{1,0:T(8,128)}, f32[8,1024]{1,0:T(8,128)}, f32[8,128]{1,0:T(8,128)}) custom-call(bf16[32,512]{1,0:T(8,128)(2,1)} %t_rows.1, bf16[16384]{0:T(1024)(128)(2,1)} %t_gain_in.1, bf16[16384,256]{1,0:T(8,128)(2,1)} %t_head.1, bf16[8,1024]{1,0:T(8,128)(2,1)} %s_rows.1, bf16[8192]{0:T(1024)(128)(2,1)} %s_gain_in.1, ...), custom_call_target="tpu_custom_call" | custom-call | flops 4294967296 | bytes 12582912 | tf_op jit(solution)/shard_map/pallas_call | solution.py:748
  100.9 1.4 %shard_map.104 = (f32[1,1]{1,0:T(1,128)}, bf16[8,1024]{1,0:T(8,128)(2,1)}, f32[8,128]{1,0:T(8,128)}) custom-call(f32[8,128]{1,0:T(8,128)} %get-tuple-element.9.loss, f32[8,1024]{1,0:T(8,128)} %get-tuple-element.10.grad, f32[8,128]{1,0:T(8,128)} %get-tuple-element.11.gain), custom_call_target="tpu_custom_call" | custom-call | tf_op jit(solution)/shard_map/pallas_call | solution.py:759

commit v4 on v3

--- a/solution.py
+++ b/solution.py
@@ -20,14 +20,15 @@
 
 
 def kernel(
-    t_rows, t_gain_in, t_head, s_rows, s_gain_in, s_head, ids, mask,
+    t_rows_in, t_gain_in, t_head, s_rows_in, s_gain_in, s_head, ids_in, mask_in,
     loss_out, grad_out, gain_out,
     g0, g1, g2, t_w, s_w, t_gain, s_gain, t_inv, s_inv, t_acc0, t_acc1, t_acc, s_acc, dot_col, lg,
     sib_out, sib_in, raf, rbf, ra_out, rb_out, ra_via, rb_via, ra_in, rb_in,
     raf2, rbf2, ra2, rb2, ra_in2, rb_in2, raf3, rbf3, ra3, rb3, ra_in3, rb_in3,
     st_c, st_p, st_z, gp_c, gp1, gp_y, gp_x, gp3, gp_z,
-    head_sem, a_send, a_recv, b_send, b_recv, ring_send, ring_recv, core_send, core_recv,
-    st_send, st_recv, sib_send_sem, sib_recv_sem, first_send, first_recv, rs_send, rs_recv, gp_send, gp_recv,
+    t_rows, t_gain_raw, s_rows, s_gain_raw, ids, mask,
+    head_sem, input_sem, a_send, a_recv, b_send, b_recv, ring_send, ring_recv, core_send, core_recv,
+    st_send, st_recv, sib_send_sem, sib_recv_sem, first_send, first_recv, rs_send, rs_recv, z_send, z_recv, gp_send, gp_recv,
 ):
     dp = lax.axis_index("dp")
     vo = lax.axis_index("vocab")
@@ -58,8 +59,21 @@
 
     t_load = pltpu.make_async_copy(t_head, t_w, head_sem.at[0])
     s_load = pltpu.make_async_copy(s_head, s_w, head_sem.at[1])
+    loads = [
+        pltpu.make_async_copy(src, dst, input_sem.at[k])
+        for k, (src, dst) in enumerate(
+            (
+                (t_rows_in, t_rows), (s_rows_in, s_rows), (t_gain_in, t_gain_raw),
+                (s_gain_in, s_gain_raw), (ids_in, ids), (mask_in, mask),
+            )
+        )
+    ]
+    for load in loads:
+        load.start()
     t_load.start()
     s_load.start()
+    for load in loads:
+        load.wait()
 
     def remote(src, dst, send, recv, to):
         return pltpu.make_async_remote_copy(
@@ -103,8 +117,8 @@
 
     squares_value = pack([t_squares, s_squares])
 
-    t_gain[...] = t_gain_in[...].astype(F32).reshape(t_gain.shape)
-    s_gain[...] = s_gain_in[...].astype(F32).reshape(s_gain.shape)
+    t_gain[...] = t_gain_raw[...].astype(F32).reshape(t_gain.shape)
+    s_gain[...] = s_gain_raw[...].astype(F32).reshape(s_gain.shape)
     for acc in (t_acc0, t_acc1, s_acc):
         acc[...] = jnp.zeros_like(acc)
 
@@ -158,13 +172,11 @@
 
         def begin(self):
             mine, theirs = self.c[1], self.b[1]
-            self.wait_a = all_partners(
-                self.a,
-                lambda j: self.g.at[c, mine, theirs, self.a[1]],
-                lambda j: self.g.at[c, mine, theirs, j],
-                lambda k: a_send.at[self.p, k],
-                lambda j: a_recv.at[self.p, j],
-            )
+            n, me, to = self.a
+            slot = self.g.at[c, mine, theirs, me]
+            for k in self.ORDER[1:]:
+                j = lax.rem(me + k, n)
+                start(slot, slot, a_send.at[self.p, k], a_recv.at[self.p, me], to(j))
 
         def row(self, core, plane, r):
             return self.g.at[core, lax.rem(self.c[1] + plane, 4), lax.rem(self.b[1] + r, 4)]
@@ -215,11 +227,30 @@
                 self.send_c(way, r, 1)
             self.cross(plane, r)
 
-        def after_a(self):
-            self.wait_a()
+        ORDER = (0, 1, 7, 2, 6, 3, 5, 4)
+
+        def after_a(self, steps):
+            n, me, to = self.a
+            for k in steps:
+                j = lax.rem(me + k, n)
+                slot = self.g.at[c, self.c[1], self.b[1], j]
+                if k:
+                    arrived(slot, a_send.at[self.p, k], a_recv.at[self.p, j], to(j))
+                for way in range(2):
+                    for send, recv, target in (
+                        (b_send, b_recv, self.to_b[way]),
+                        (ring_send, ring_recv, self.to_c[way]),
+                    ):
+                        remote(slot, slot, send.at[self.p, way, 0], recv.at[self.p, way, 0], target).start()
+
+        def row_sent(self):
+            row = self.row(c, 0, 0)
             for way in range(2):
-                self.send_b(way, 0)
-                self.send_c(way, 0)
+                for send, recv, target in (
+                    (b_send, b_recv, self.to_b[way]),
+                    (ring_send, ring_recv, self.to_c[way]),
+                ):
+                    late.append(remote(row, row, send.at[self.p, way, 0], recv.at[self.p, way, 0], target))
             self.cross(0, 0)
 
     class Ring:
@@ -333,12 +364,16 @@
         lambda k: a_send.at[0, k],
         lambda j: a_recv.at[0, j],
     )
-    next(round0)
-    next(round0)
+    for part in both:
+        part.after_a(Rows.ORDER[:1])
+    part1.after_a(Rows.ORDER[1:])
     wait_plane()
     part0.begin()
-    for part in both:
-        part.after_a()
+    next(round0)
+    part2.after_a(Rows.ORDER[1:])
+    next(round0)
+    for part in both:
+        part.row_sent()
     part0.event(0)
     for part in both:
         part.take_b(0)
@@ -525,22 +560,20 @@
             lax.fori_loop(0, 16, step, 0, unroll=4)
             self.send(way, 2)
 
-        def last(self, total, out):
-            for way in range(2):
-                self.take(way, 1)
-                self.take(way, 2)
-
-            def step(i, carry):
-                row, zl_ = lax.div(i, 4), lax.rem(i, 4)
-                for zh_ in range(2):
-                    value = self.own[self.me, zh_, row, zl_] + (
-                        self.landing[0, zh_, row, zl_].astype(F32) + self.landing[1, zh_, row, zl_].astype(F32)
+        def last(self, half, total, out):
+            self.take(1 - half, 1)
+            self.take(half, 2)
+
+            def step(row, carry):
+                for zl_ in range(4):
+                    value = self.own[self.me, half, row, zl_] + (
+                        self.landing[0, half, row, zl_].astype(F32) + self.landing[1, half, row, zl_].astype(F32)
                     )
-                    total[row, zh_ * 4 + zl_] = value
-                    out[row, zh_ * 4 + zl_] = value.astype(BF16)
+                    total[row, half, zl_] = value
+                    out[row, half, zl_] = value.astype(BF16)
                 return carry
 
-            lax.fori_loop(0, 16, step, 0, unroll=2)
+            lax.fori_loop(0, 4, step, 0)
 
     first_a = First(0, axis_x, raf, ra_out, ra_via, ra_in)
     first_b = First(1, axis_y, rbf, rb_out, rb_via, rb_in)
@@ -575,6 +608,48 @@
         gp_c[c, y_, zh_] = jnp.concatenate(pieces, axis=0)
         return carry
 
+    def scatter(axis, src, landing, part, half):
+        return all_partners(
+            axis,
+            lambda j: src.at[j, half],
+            lambda j: landing.at[j, half],
+            lambda k: rs_send.at[part, half, k],
+            lambda j: rs_recv.at[part, half, j],
+        )
+
+    def second_sum(axis, half, own, landing, total, out):
+        n, me, _ = axis
+        for at in range(4):
+            value = own[me, half, at]
+            for k in range(1, n):
+                value = value + landing[lax.rem(me + k, n), half, at].astype(F32)
+            total[half * 4 + at] = value
+            out[half * 4 + at] = value.astype(BF16)
+
+    own_sends = []
+
+    def send_z(half, src, landing, part):
+        for k in range(4):
+            j = half * 4 + lax.rem(zl + k, 4)
+            copy = remote(
+                src.at[j], landing.at[z], z_send.at[part, half, k], z_recv.at[part, z], to_z(j)
+            )
+            if k:
+                copy.start()
+                late.append(copy)
+            else:
+                pl.when(zh != half)(copy.start)
+                own_sends.append((half, copy))
+
+    def third_sum(own, landing, part):
+        for k in range(1, Z):
+            j = lax.rem(z + k, Z)
+            arrived(landing.at[j], z_send.at[part, 0, 1], z_recv.at[part, j], to_z(j))
+        value = own[z]
+        for k in range(1, Z):
+            value = value + landing[lax.rem(z + k, Z)].astype(F32)
+        return value
+
     lax.fori_loop(0, 4, gain_step, 0)
     first_b.middle(0)
     first_a.middle(0)
@@ -584,41 +659,26 @@
     )
     first_b.middle(1)
     first_a.middle(1)
+    first_b.last(0, rbf2, rb2)
+    wait_b0 = scatter(axis_x, rb2, rb_in2, 1, 0)
+    first_a.last(0, raf2, ra2)
+    wait_a0 = scatter(axis_y, ra2, ra_in2, 0, 0)
     gain_wait()
     gp1[...] = gp_c[0] + gp_c[1]
     gp_y[y] = gp1[y]
     gain_wait = all_partners(
         axis_y, lambda j: gp1.at[j], lambda j: gp_y.at[j], lambda k: gp_send.at[1, k], lambda j: gp_recv.at[1, j]
     )
-
-    def scatter(axis, src, landing, part, phase):
-        return all_partners(
-            axis,
-            lambda j: src.at[j],
-            lambda j: landing.at[j],
-            lambda k: rs_send.at[part, phase, k],
-            lambda j: rs_recv.at[part, phase, j],
-        )
-
-    def second_sum(axis, own, landing, total, out):
-        n, me, _ = axis
-        for at in range(Z):
-            value = own[me, at]
-            for k in range(1, n):
-                value = value + landing[lax.rem(me + k, n), at].astype(F32)
-            total[at] = value
-            out[at] = value.astype(BF16)
-
-    def third_sum(own, landing):
-        value = own[z]
-        for k in range(1, Z):
-            value = value + landing[lax.rem(z + k, Z)].astype(F32)
-        return value
-
-    first_a.last(raf2, ra2)
-    wait_a = scatter(axis_y, ra2, ra_in2, 0, 0)
-    first_b.last(rbf2, rb2)
-    wait_b = scatter(axis_x, rb2, rb_in2, 1, 0)
+    first_b.last(1, rbf2, rb2)
+    wait_b1 = scatter(axis_x, rb2, rb_in2, 1, 1)
+    first_a.last(1, raf2, ra2)
+    wait_a1 = scatter(axis_y, ra2, ra_in2, 0, 1)
+    wait_b0()
+    second_sum(axis_x, 0, rbf2, rb_in2, rbf3, rb3)
+    send_z(0, rb3, rb_in3, 1)
+    wait_a0()
+    second_sum(axis_y, 0, raf2, ra_in2, raf3, ra3)
+    send_z(0, ra3, ra_in3, 0)
     gain_wait()
     gp_x[x] = add_all([gp_y[j] for j in range(Y)])
     gain_wait = all_partners(
@@ -630,12 +690,12 @@
     loss = jnp.sum(unpack(second, 0), axis=1, keepdims=True) / count
     loss_out[...] = jnp.broadcast_to(loss, loss_out.shape)
 
-    wait_a()
-    second_sum(axis_y, raf2, ra_in2, raf3, ra3)
-    wait_a = scatter(axis_z, ra3, ra_in3, 0, 1)
-    wait_b()
-    second_sum(axis_x, rbf2, rb_in2, rbf3, rb3)
-    wait_b = scatter(axis_z, rb3, rb_in3, 1, 1)
+    wait_b1()
+    second_sum(axis_x, 1, rbf2, rb_in2, rbf3, rb3)
+    send_z(1, rb3, rb_in3, 1)
+    wait_a1()
+    second_sum(axis_y, 1, raf2, ra_in2, raf3, ra3)
+    send_z(1, ra3, ra_in3, 0)
     gain_wait()
     gp3[...] = add_all([gp_x[j] for j in range(X)])
     gp_z[z] = gp3[zh]
@@ -646,9 +706,7 @@
         lambda k: gp_send.at[3, k],
         lambda j: gp_recv.at[3, j],
     )
-    wait_a()
-    wait_b()
-    normed_grad = jnp.concatenate([third_sum(raf3, ra_in3), third_sum(rbf3, rb_in3)], axis=1)
+    normed_grad = jnp.concatenate([third_sum(raf3, ra_in3, 0), third_sum(rbf3, rb_in3, 1)], axis=1)
     inv = wide(s_inv[lax.div(dp, 2), c])
     dots = wide(dot_col[lax.div(dp, 2), c])
     for h in range(2):
@@ -660,6 +718,8 @@
     gain_out[...] = add_all([gp_z[j] for j in range(Z)])
     for copy in late:
         copy.wait_send()
+    for half, copy in own_sends:
+        pl.when(zh != half)(copy.wait_send)
 
 
 def results(loss, grad, gain, loss_out, grad_out, gain_out):
@@ -698,12 +758,12 @@
         pltpu.VMEM((2, 4, 4, 16, 256), BF16),
         pltpu.VMEM((2, 2, Y, 4, 16, 256), BF16),
         pltpu.VMEM((2, 2, X, 4, 16, 256), BF16),
-        pltpu.VMEM((Y, Z, 16, 256), F32),
-        pltpu.VMEM((X, Z, 16, 256), F32),
-        pltpu.VMEM((Y, Z, 16, 256), BF16),
-        pltpu.VMEM((X, Z, 16, 256), BF16),
-        pltpu.VMEM((Y, Z, 16, 256), BF16),
-        pltpu.VMEM((X, Z, 16, 256), BF16),
+        pltpu.VMEM((Y, 2, 4, 16, 256), F32),
+        pltpu.VMEM((X, 2, 4, 16, 256), F32),
+        pltpu.VMEM((Y, 2, 4, 16, 256), BF16),
+        pltpu.VMEM((X, 2, 4, 16, 256), BF16),
+        pltpu.VMEM((Y, 2, 4, 16, 256), BF16),
+        pltpu.VMEM((X, 2, 4, 16, 256), BF16),
         pltpu.VMEM((Z, 16, 256), F32),
         pltpu.VMEM((Z, 16, 256), F32),
         pltpu.VMEM((Z, 16, 256), BF16),
@@ -719,7 +779,14 @@
         pltpu.VMEM((X, 2, 8, 128), F32),
         pltpu.VMEM((2, 8, 128), F32),
         pltpu.VMEM((Z, 8, 128), F32),
+        pltpu.VMEM(t_rows.shape, BF16),
+        pltpu.VMEM(t_gain.shape, BF16),
+        pltpu.VMEM(s_rows.shape, BF16),
+        pltpu.VMEM(s_gain.shape, BF16),
+        pltpu.VMEM((1, TOKENS), jnp.int32),
+        pltpu.VMEM((1, TOKENS), jnp.int32),
         dma((2,)),
+        dma((6,)),
         dma((3, 16)),
         dma((3, 16)),
         dma((3, 2, 2)),
@@ -734,8 +801,10 @@
         dma((8,)),
         dma((2, 2, 3)),
         dma((2, 2, 3)),
-        dma((2, 2, 8)),
-        dma((2, 2, 8)),
+        dma((2, 2, 4)),
+        dma((2, 2, 4)),
+        dma((2, 2, 4)),
+        dma((2, 8)),
         dma((4, 8)),
         dma((4, 8)),
     ]
@@ -748,7 +817,7 @@
     values = pl.pallas_call(
         kernel,
         out_shape=shapes,
-        in_specs=[vmem, vmem, hbm, vmem, vmem, hbm, vmem, vmem],
+        in_specs=[hbm] * 8,
         out_specs=(vmem, vmem, vmem),
         scratch_shapes=scratch,
         compiler_params=pltpu.CompilerParams(

time: 103 us -> 101 us (0.981)
  Pallas kernels: 102 us -> 99.7 us
    pallas_call x1, Pallas kernels: 100 us -> 98.3 us  [shards(): pl.pallas_call(kernel, out_shape=shapes, in_specs=[hbm] * 8, out_specs=(v...]
where the time goes in v4:
time: 101 us; the launch traced here: 100 us
  Pallas kernels  99.7 us (99%)
    pallas_call x1, Pallas kernels, shards(): pl.pallas_call(kernel, out_shape=shapes, in_specs=[hbm] * 8, out_specs=(v...  98.3 us

profile of v4, /device:TPU:32, one launch (start us, length us, event | category | flops | bytes accessed | tf_op | source)
XLA Modules:
  0.0 100.3 jit_solution(7940304158614362276)
XLA Ops:
  0.6 98.3 %shard_map.103 = (f32[8,128]{1,0:T(8,128)}, f32[8,1024]{1,0:T(8,128)}, f32[8,128]{1,0:T(8,128)}) custom-call(bf16[32,512]{1,0:T(8,128)(2,1)} %t_rows_in.1, bf16[16384]{0:T(1024)(128)(2,1)} %t_gain_in.1, bf16[16384,256]{1,0:T(8,128)(2,1)} %t_head.1, bf16[8,1024]{1,0:T(8,128)(2,1)} %s_rows_in.1, bf16[8192]{0:T(1024)(128)(2,1)} %s_gain_in.1, ...), custom_call_target="tpu_custom_call" | custom-call | flops 4294967296 | bytes 12582912 | tf_op jit(solution)/shard_map/pallas_call | solution.py:817
  99.0 1.4 %shard_map.104 = (f32[1,1]{1,0:T(1,128)}, bf16[8,1024]{1,0:T(8,128)(2,1)}, f32[8,128]{1,0:T(8,128)}) custom-call(f32[8,128]{1,0:T(8,128)} %get-tuple-element.9.loss, f32[8,1024]{1,0:T(8,128)} %get-tuple-element.10.grad, f32[8,128]{1,0:T(8,128)} %get-tuple-element.11.gain), custom_call_target="tpu_custom_call" | custom-call | tf_op jit(solution)/shard_map/pallas_call | solution.py:828

commit v5 on v4

--- a/solution.py
+++ b/solution.py
@@ -650,12 +650,17 @@
             value = value + landing[lax.rem(z + k, Z)].astype(F32)
         return value
 
-    lax.fori_loop(0, 4, gain_step, 0)
+    lax.fori_loop(0, 8, gain_step, 0)
+    gain_wait = all_partners(
+        axis_c, lambda j: gp_c.at[c], lambda j: gp_c.at[j], lambda k: gp_send.at[0, k], lambda j: gp_recv.at[0, j]
+    )
     first_b.middle(0)
     first_a.middle(0)
-    lax.fori_loop(4, 8, gain_step, 0)
+    gain_wait()
+    gp1[...] = gp_c[0] + gp_c[1]
+    gp_y[y] = gp1[y]
     gain_wait = all_partners(
-        axis_c, lambda j: gp_c.at[c], lambda j: gp_c.at[j], lambda k: gp_send.at[0, k], lambda j: gp_recv.at[0, j]
+        axis_y, lambda j: gp1.at[j], lambda j: gp_y.at[j], lambda k: gp_send.at[1, k], lambda j: gp_recv.at[1, j]
     )
     first_b.middle(1)
     first_a.middle(1)
@@ -664,10 +669,9 @@
     first_a.last(0, raf2, ra2)
     wait_a0 = scatter(axis_y, ra2, ra_in2, 0, 0)
     gain_wait()
-    gp1[...] = gp_c[0] + gp_c[1]
-    gp_y[y] = gp1[y]
+    gp_x[x] = add_all([gp_y[j] for j in range(Y)])
     gain_wait = all_partners(
-        axis_y, lambda j: gp1.at[j], lambda j: gp_y.at[j], lambda k: gp_send.at[1, k], lambda j: gp_recv.at[1, j]
+        axis_x, lambda j: gp_x.at[x], lambda j: gp_x.at[j], lambda k: gp_send.at[2, k], lambda j: gp_recv.at[2, j]
     )
     first_b.last(1, rbf2, rb2)
     wait_b1 = scatter(axis_x, rb2, rb_in2, 1, 1)
@@ -679,23 +683,7 @@
     wait_a0()
     second_sum(axis_y, 0, raf2, ra_in2, raf3, ra3)
     send_z(0, ra3, ra_in3, 0)
-    gain_wait()
-    gp_x[x] = add_all([gp_y[j] for j in range(Y)])
-    gain_wait = all_partners(
-        axis_x, lambda j: gp_x.at[x], lambda j: gp_x.at[j], lambda k: gp_send.at[2, k], lambda j: gp_recv.at[2, j]
-    )
-
-    row_dot = row_scale * (unpack(second, 2) - rest * kl * unpack(second, 3)) / DS
-    dot_col[...] = column(row_dot).reshape(dot_col.shape)
-    loss = jnp.sum(unpack(second, 0), axis=1, keepdims=True) / count
-    loss_out[...] = jnp.broadcast_to(loss, loss_out.shape)
-
-    wait_b1()
-    second_sum(axis_x, 1, rbf2, rb_in2, rbf3, rb3)
-    send_z(1, rb3, rb_in3, 1)
-    wait_a1()
-    second_sum(axis_y, 1, raf2, ra_in2, raf3, ra3)
-    send_z(1, ra3, ra_in3, 0)
+
     gain_wait()
     gp3[...] = add_all([gp_x[j] for j in range(X)])
     gp_z[z] = gp3[zh]
@@ -706,6 +694,17 @@
         lambda k: gp_send.at[3, k],
         lambda j: gp_recv.at[3, j],
     )
+    row_dot = row_scale * (unpack(second, 2) - rest * kl * unpack(second, 3)) / DS
+    dot_col[...] = column(row_dot).reshape(dot_col.shape)
+    loss = jnp.sum(unpack(second, 0), axis=1, keepdims=True) / count
+    loss_out[...] = jnp.broadcast_to(loss, loss_out.shape)
+
+    wait_b1()
+    second_sum(axis_x, 1, rbf2, rb_in2, rbf3, rb3)
+    send_z(1, rb3, rb_in3, 1)
+    wait_a1()
+    second_sum(axis_y, 1, raf2, ra_in2, raf3, ra3)
+    send_z(1, ra3, ra_in3, 0)
     normed_grad = jnp.concatenate([third_sum(raf3, ra_in3, 0), third_sum(rbf3, rb_in3, 1)], axis=1)
     inv = wide(s_inv[lax.div(dp, 2), c])
     dots = wide(dot_col[lax.div(dp, 2), c])

time: 101 us -> 98.2 us (0.972)
  Pallas kernels: 99.7 us -> 96.8 us
    pallas_call x1, Pallas kernels: 98.3 us -> 95.4 us  [shards(): pl.pallas_call(kernel, out_shape=shapes, in_specs=[hbm] * 8, out_specs=(v...]
where the time goes in v5:
time: 98.2 us; the launch traced here: 97.4 us
  Pallas kernels  96.8 us (99%)
    pallas_call x1, Pallas kernels, shards(): pl.pallas_call(kernel, out_shape=shapes, in_specs=[hbm] * 8, out_specs=(v...  95.4 us

profile of v5, /device:TPU:32, one launch (start us, length us, event | category | flops | bytes accessed | tf_op | source)
XLA Modules:
  0.0 97.4 jit_solution(10748281974110042093)
XLA Ops:
  0.6 95.4 %shard_map.103 = (f32[8,128]{1,0:T(8,128)}, f32[8,1024]{1,0:T(8,128)}, f32[8,128]{1,0:T(8,128)}) custom-call(bf16[32,512]{1,0:T(8,128)(2,1)} %t_rows_in.1, bf16[16384]{0:T(1024)(128)(2,1)} %t_gain_in.1, bf16[16384,256]{1,0:T(8,128)(2,1)} %t_head.1, bf16[8,1024]{1,0:T(8,128)(2,1)} %s_rows_in.1, bf16[8192]{0:T(1024)(128)(2,1)} %s_gain_in.1, ...), custom_call_target="tpu_custom_call" | custom-call | flops 4294967296 | bytes 12582912 | tf_op jit(solution)/shard_map/pallas_call | solution.py:816
  96.0 1.4 %shard_map.104 = (f32[1,1]{1,0:T(1,128)}, bf16[8,1024]{1,0:T(8,128)(2,1)}, f32[8,128]{1,0:T(8,128)}) custom-call(f32[8,128]{1,0:T(8,128)} %get-tuple-element.9.loss, f32[8,1024]{1,0:T(8,128)} %get-tuple-element.10.grad, f32[8,128]{1,0:T(8,128)} %get-tuple-element.11.gain), custom_call_target="tpu_custom_call" | custom-call | tf_op jit(solution)/shard_map/pallas_call | solution.py:827

commit v6 on v5

--- a/solution.py
+++ b/solution.py
@@ -320,7 +320,7 @@
             s_acc[...] = total
             return carry
 
-        lax.fori_loop(0, 2 * count, step, 0)
+        lax.fori_loop(0, 2 * count, step, 0, unroll=2)
 
     def teacher_step(acc, p, load, first, count):
         lhs = []
@@ -341,7 +341,7 @@
             teacher_step(t_acc1, 1, load, (zl_ * X + x_) * 2, 2)
             return carry
 
-        lax.fori_loop(0, 4 * count, step, 0, unroll=2)
+        lax.fori_loop(0, 4 * count, step, 0, unroll=4)
 
     def teacher_z(count, plane_of):
         def step(i, carry):
@@ -350,7 +350,7 @@
             teacher_step(t_acc0, 0, load, (zl_ * X + x_) * 2, 4)
             return carry
 
-        lax.fori_loop(0, 2 * count, step, 0)
+        lax.fori_loop(0, 2 * count, step, 0, unroll=2)
 
     squares = []
     round0 = exchange(0, squares_value, add_all, squares, (over_z, over_c, over_p))

time: 98.2 us -> 98 us (level)
  no operation moved by 1% of the time
where the time goes in v6:
time: 98 us; the launch traced here: 97.8 us
  Pallas kernels  97.2 us (99%)
    pallas_call x1, Pallas kernels, shards(): pl.pallas_call(kernel, out_shape=shapes, in_specs=[hbm] * 8, out_specs=(v...  95.8 us

profile of v6, /device:TPU:32, one launch (start us, length us, event | category | flops | bytes accessed | tf_op | source)
XLA Modules:
  0.0 97.8 jit_solution(2571502072248741214)
XLA Ops:
  0.6 95.8 %shard_map.103 = (f32[8,128]{1,0:T(8,128)}, f32[8,1024]{1,0:T(8,128)}, f32[8,128]{1,0:T(8,128)}) custom-call(bf16[32,512]{1,0:T(8,128)(2,1)} %t_rows_in.1, bf16[16384]{0:T(1024)(128)(2,1)} %t_gain_in.1, bf16[16384,256]{1,0:T(8,128)(2,1)} %t_head.1, bf16[8,1024]{1,0:T(8,128)(2,1)} %s_rows_in.1, bf16[8192]{0:T(1024)(128)(2,1)} %s_gain_in.1, ...), custom_call_target="tpu_custom_call" | custom-call | flops 4294967296 | bytes 12582912 | tf_op jit(solution)/shard_map/pallas_call | solution.py:816
  96.4 1.4 %shard_map.104 = (f32[1,1]{1,0:T(1,128)}, bf16[8,1024]{1,0:T(8,128)(2,1)}, f32[8,128]{1,0:T(8,128)}) custom-call(f32[8,128]{1,0:T(8,128)} %get-tuple-element.9.loss, f32[8,1024]{1,0:T(8,128)} %get-tuple-element.10.grad, f32[8,128]{1,0:T(8,128)} %get-tuple-element.11.gain), custom_call_target="tpu_custom_call" | custom-call | tf_op jit(solution)/shard_map/pallas_call | solution.py:827
